TPU v7x, 512 devices: a whole 4x4x16 slice. The times are simulated.
512 devices in a mesh: cp: 32 (over z, x_hi), tp: 4 (over x_lo, core), dp: 4 (over y).
Axes of the slice: x: 4 (x_hi: 2, x_lo: 2; x = x_hi * 2 + x_lo), y: 4, z: 16, core: 2. Of those that a mesh axis runs over, the one named last changes fastest.
Arguments:
- q_proj: bfloat16 [4096, 4096], P('cp', ('tp', 'dp')), may hold values from -18 to 18
- key_projection: bfloat16 [4096, 256], P('cp'), may hold values from -18 to 18
- value_projection: bfloat16 [4096, 256], P('cp'), may hold values from -6 to 6
- segments: int32 [4096], replicated, may hold values from 0 to 7, never falling along the last dimension, each value on 1 to 2048 neighbouring positions
- resid: bfloat16 [4096, 4096], P('cp', ('tp', 'dp')), may hold values from -6 to 6
- norm_gain: bfloat16 [4096], replicated, may hold values from 0.5 to 1.5
- route_ids: int32 [4096, 8], P(('cp', 'dp')), may hold values from 0 to 127, all different within a row; in each aligned block of 32 rows (0 to 31, 32 to 63, ...) at most 4 rows name the same one
- route_gates: float32 [4096, 8], P(('cp', 'dp')), may hold values from 0.05 to 0.5
- w_gate: bfloat16 [128, 768, 4096], P(('cp', 'dp'), 'tp'), may hold values from -0.09375 to 0.09375
- w_up: bfloat16 [128, 768, 4096], P(('cp', 'dp'), 'tp'), may hold values from -0.09375 to 0.09375
- w_down: bfloat16 [128, 768, 4096], P(('cp', 'dp'), None, 'tp'), may hold values from -0.21875 to 0.21875
Outputs:
- mixed: bfloat16 [4096, 4096], P(('cp', 'dp'), 'tp')
Inputs may be any that keep to these rules, and one draw needn't show every extreme that they name: `route_ids`: each row names 8 different experts; in each aligned block of 32 rows no expert is named by more than 4 rows, and in every block some expert is named by exactly 4. `segments`: document numbers never fall along the sequence; a document spans 1 to 2048 positions, one exactly that many.
All inputs are finite; a program needn't handle non-finite values.
Results may differ from a plain program's by a relative error of at most 0.006.
Values may be sent and summed in bfloat16 or wider, within the bound.
A program may use at most 64 MiB of HBM per device.

v0:
```python
import jax
import jax.numpy as jnp
from jax import lax
from jax.sharding import PartitionSpec as P

QUERY_HEADS = 32
KEY_VALUE_HEADS = 2
HEAD_WIDTH = 128


epsilon = 1e-06
masked_score = -1e30


def slot_targets(route_ids, expert_count, capacity):
    flat_ids = route_ids.reshape(-1)
    one_hot = (flat_ids[:, None] == jnp.arange(expert_count, dtype=jnp.int32)[None, :]).astype(
        jnp.int32
    )
    slot_number = jnp.sum((jnp.cumsum(one_hot, 0) - one_hot) * one_hot, 1)
    return flat_ids * capacity + slot_number


def fill_slots(targets, tokens_in, slot_count, top_count):
    picker = (targets[None, :] == jnp.arange(slot_count, dtype=jnp.int32)[:, None]).astype(
        jnp.bfloat16
    )
    picker = picker.reshape(slot_count, tokens_in.shape[0], top_count).sum(2)
    return jnp.dot(picker, tokens_in, preferred_element_type=jnp.float32).astype(jnp.bfloat16)


def combine_slots(returned, targets, gate_values, residual_part):
    width_here = returned.shape[-1]
    flat_out = returned.reshape(-1, width_here)
    picked = jnp.take(flat_out, targets, axis=0).reshape(
        gate_values.shape[0], gate_values.shape[1], width_here
    )
    expert_sum = jnp.einsum("rj,rjd->rd", gate_values, picked.astype(jnp.float32))
    return (residual_part.astype(jnp.float32) + expert_sum).astype(jnp.bfloat16)


def body(
    q_proj,
    key_projection,
    value_projection,
    segments,
    resid,
    norm_gain,
    route_ids,
    route_gates,
    w_gate,
    w_up,
    w_down,
):
    n_tensor = lax.axis_size("tp")
    n_data = lax.axis_size("dp")
    n_context = lax.axis_size("cp")
    tensor_index = lax.axis_index("tp")
    data_index = lax.axis_index("dp")
    context_index = lax.axis_index("cp")
    row_count = q_proj.shape[0]
    count_of_heads = q_proj.shape[1] // HEAD_WIDTH
    top_count = route_ids.shape[1]
    head_slab = tensor_index * n_data + data_index
    key_value_head = head_slab * count_of_heads // (QUERY_HEADS // KEY_VALUE_HEADS)
    k_mine = lax.dynamic_slice_in_dim(key_projection, key_value_head * HEAD_WIDTH, HEAD_WIDTH, 1)
    v_mine = lax.dynamic_slice_in_dim(value_projection, key_value_head * HEAD_WIDTH, HEAD_WIDTH, 1)
    first_row = context_index * row_count
    seg_mine = lax.dynamic_slice_in_dim(segments, first_row, row_count, 0)
    q_positions = first_row + jnp.arange(row_count, dtype=jnp.int32)
    q_heads = q_proj.reshape(row_count, count_of_heads, HEAD_WIDTH)
    score_scale = HEAD_WIDTH ** (-0.5)
    begin_state = (
        jnp.full((count_of_heads, row_count), masked_score, jnp.float32),
        jnp.zeros((count_of_heads, row_count), jnp.float32),
        jnp.zeros((count_of_heads, row_count, HEAD_WIDTH), jnp.float32),
    )
    shard_piece = (
        lax.all_gather(k_mine, "cp", axis=0, tiled=True),
        lax.all_gather(v_mine, "cp", axis=0, tiled=True),
    )

    def attend_piece(running_state):
        run_max, run_total, run_acc = running_state
        k_piece, v_piece = shard_piece
        key_count = k_piece.shape[0]
        k_positions = jnp.arange(key_count, dtype=jnp.int32)
        allowed = (k_positions[None, :] <= q_positions[:, None]) & (
            segments[None, :] == seg_mine[:, None]
        )
        scores = (
            jnp.einsum("rhd,kd->hrk", q_heads, k_piece, preferred_element_type=jnp.float32)
            * score_scale
        )
        scores = jnp.where(allowed[None], scores, masked_score)
        new_max = jnp.maximum(run_max, jnp.max(scores, 2))
        weights = jnp.exp(scores - new_max[:, :, None])
        new_total = jnp.sum(weights, 2)
        mixed_values = jnp.einsum(
            "hrk,kd->hrd", weights.astype(jnp.bfloat16), v_piece, preferred_element_type=jnp.float32
        )
        return (new_max, new_total, mixed_values)

    final_max, final_total, final_acc = lax.cond(
        jnp.int32(0) <= first_row + row_count - 1,
        attend_piece,
        lambda running_state: running_state,
        begin_state,
    )
    attended = (
        (final_acc / final_total[:, :, None])
        .transpose(1, 0, 2)
        .reshape(row_count, count_of_heads * HEAD_WIDTH)
    )
    after_attn = (resid.astype(jnp.float32) + attended).astype(jnp.bfloat16)
    folded = lax.all_to_all(after_attn, "dp", split_axis=0, concat_axis=1, tiled=True)
    col_count = folded.shape[1]
    values = folded.astype(jnp.float32)
    squares = lax.psum(jnp.sum(values * values, 1), "tp")
    inverse = lax.rsqrt(squares / (col_count * n_tensor) + epsilon)[:, None]
    gain_here = lax.dynamic_slice_in_dim(norm_gain, tensor_index * col_count, col_count, 0)
    normed = (values * inverse * gain_here.astype(jnp.float32)).astype(jnp.bfloat16)
    expert_count = n_context * n_data
    device_rows = folded.shape[0]
    capacity = max(2, min(device_rows, 2 * device_rows * top_count // expert_count))
    slot_total = expert_count * capacity
    targets = slot_targets(route_ids, expert_count, capacity)
    gate_rows = w_gate[0]
    up_rows = w_up[0]
    down_rows = w_down[0]
    contract = (((1,), (1,)), ((), ()))
    full = lax.all_gather(normed, "tp", axis=1, tiled=True)
    outgoing = fill_slots(targets, full, slot_total, top_count).reshape(
        expert_count, capacity, full.shape[1]
    )
    arrived = lax.all_to_all(
        outgoing, ("cp", "dp"), split_axis=0, concat_axis=0, tiled=True
    ).reshape(slot_total, full.shape[1])
    gate_val = lax.dot_general(arrived, gate_rows, contract, preferred_element_type=jnp.float32)
    up_val = lax.dot_general(arrived, up_rows, contract, preferred_element_type=jnp.float32)
    hidden = (jax.nn.silu(gate_val) * up_val).astype(jnp.bfloat16)
    produced = jnp.dot(
        lax.all_gather(hidden, "tp", axis=1, tiled=True),
        down_rows,
        preferred_element_type=jnp.float32,
    ).astype(jnp.bfloat16)
    returned = lax.all_to_all(
        produced.reshape(expert_count, capacity, down_rows.shape[1]),
        ("cp", "dp"),
        split_axis=0,
        concat_axis=0,
        tiled=True,
    )
    return combine_slots(returned, targets, route_gates, folded)


def solution(mesh):
    placed = (
        P("cp", ("tp", "dp")),
        P("cp", None),
        P("cp", None),
        P(),
        P("cp", ("tp", "dp")),
        P(),
        P(("cp", "dp"), None),
        P(("cp", "dp"), None),
        P(("cp", "dp"), "tp", None),
        P(("cp", "dp"), "tp", None),
        P(("cp", "dp"), None, "tp"),
    )
    return jax.shard_map(
        body, mesh=mesh, in_specs=placed, out_specs=P(("cp", "dp"), "tp"), check_vma=False
    )
```

profile of v0, /device:TPU:6, one launch (start us, length us, event | category | flops | bytes accessed | tf_op | source)
XLA Modules:
  0.0 637.1 jit_solution(8440918521292634723)
XLA Ops:
  6.5 1.5 constant_dynamic-slice_fusion.1
  8.1 1.4 constant_dynamic-slice_fusion
  9.5 0.8 copy.56
  10.4 1.0 copy.52
  12.4 144.0 %all-gather.3.cloned.1.call-done = bf16[4096,128]{1,0:T(8,128)(2,1)} async-done(((bf16[128,128]{1,0:T(8,128)(2,1)}), bf16[4096,128]{1,0:T(8,128)(2,1)}) %all-gather.3.cloned.1.call-update) | async-done | bytes 1048592 | tf_op jit(solution)/shard_map/all_gather | solution.py:79
  156.3 140.3 %all-gather.5.cloned.1.call-done = bf16[4096,128]{1,0:T(8,128)(2,1)} async-done(((bf16[128,128]{1,0:T(8,128)(2,1)}), bf16[4096,128]{1,0:T(8,128)(2,1)}) %all-gather.5.cloned.1.call-update) | async-done | bytes 1048592 | tf_op jit(solution)/shard_map/all_gather | solution.py:80
  296.7 6.9 %conditional.1 = (f32[2,128]{1,0:T(2,128)S(1)}, f32[2,128,128]{1,2,0:T(8,128)S(1)}) conditional(s32[]{:T(128)} %convert_element_type.60, () %tuple.15, (s32[]{:T(128)}, s32[128]{0:T(128)S(1)}, s32[4096]{0:T(1024)}, bf16[128,256]{1,0:T(8,128)(2,1)}, bf16[4096,128]{1,0:T(8,128)(2,1)}, /*index=5*/bf16[4096,128]{1,0:T(8,128)(2,1)}) %tuple.16), branch_computations={%region_0.1_spmd, %region_1.4_spmd} | conditional | flops 545783680 | bytes 20145238 | solution.py:104
  296.7 0.9 dynamic_slice.10
  297.5 2.5 fusion.7
  300.0 2.1 fusion.43
  302.1 0.8 fusion.4
  303.0 0.6 fusion.3
  303.6 0.7 copy.54
  304.3 4.3 all-to-all-start
  308.6 0.7 dynamic-slice_convert_fusion
  309.3 4.9 all-to-all-done
  314.4 5.8 psum.7
  320.3 5.8 all_gather.14
  326.0 3.2 convolution_convert_fusion
  329.3 7.2 %reshape.160 = bf16[128,4,4096]{2,1,0:T(4,128)(2,1)} reshape(bf16[512,4096]{1,0:T(8,128)(2,1)} %convolution_convert_fusion) | data formatting | bytes 8388608 | tf_op jit(solution)/shard_map/reshape | solution.py:133
  336.5 198.5 %all_to_all.23 = bf16[128,4,4096]{2,1,0:T(4,128)(2,1)} all-to-all(bf16[128,4,4096]{2,1,0:T(4,128)(2,1)} %reshape.160), channel_id=1, replica_groups=mesh['cp'=32,'tp'=4,'dp'=4] {'cp','dp'}, dimensions={0} | all-to-all | bytes 8388608 | tf_op jit(solution)/shard_map/all_to_all | solution.py:136
  535.0 6.9 %reshape.161 = bf16[512,4096]{1,0:T(8,128)(2,1)} reshape(bf16[128,4,4096]{2,1,0:T(4,128)(2,1)} %all_to_all.23) | data formatting | bytes 8388608 | tf_op jit(solution)/shard_map/reshape | solution.py:138
  541.9 4.3 fusion.16
  546.3 1.5 fusion.24
  547.8 7.6 %all_gather.15 = bf16[512,768]{0,1:T(8,128)(2,1)S(1)} all-gather(bf16[512,192]{0,1:T(8,128)(2,1)S(1)} %fusion.24), channel_id=1, replica_groups=mesh['cp'=32,'tp'=4,'dp'=4] {'tp'}, dimensions={1}, use_global_device_ids=true | all-gather | bytes 983040 | tf_op jit(solution)/shard_map/all_gather | solution.py:143
  555.4 1.0 fusion.18
  556.4 1.2 reshape.162
  557.7 13.9 %all-to-all-start.2 = ((bf16[128,4,1024]{2,1,0:T(4,128)(2,1)}), bf16[128,4,1024]{2,1,0:T(4,128)(2,1)}, u32[]{:S(2)}, u32[]{:S(2)}) async-start(bf16[128,4,1024]{2,1,0:T(4,128)(2,1)} %reshape.162), calls=%async_computation.2 | async-start | bytes 2097152 | tf_op jit(solution)/shard_map/all_to_all | solution.py:147
  571.8 54.9 %all-to-all-done.2 = bf16[128,4,1024]{2,1,0:T(4,128)(2,1)} async-done(((bf16[128,4,1024]{2,1,0:T(4,128)(2,1)}), bf16[128,4,1024]{2,1,0:T(4,128)(2,1)}, u32[]{:S(2)}, u32[]{:S(2)}) %all-to-all-start.2) | async-done | bytes 1048608 | tf_op jit(solution)/shard_map/all_to_all | solution.py:147
  626.7 1.3 reshape.163
  628.1 1.2 gather_fusion
  629.6 0.7 fusion.37
  (44 shorter events, 2.0 us)
Async XLA Ops:
  6.5 548.9 %copy-start = (bf16[1,768,1024]{2,1,0:T(8,128)(2,1)S(1)}, bf16[1,768,1024]{2,1,0:T(8,128)(2,1)}, u32[]{:S(2)}) copy-start(bf16[1,768,1024]{2,1,0:T(8,128)(2,1)} %param.23) | copy-start | bytes 4718596
  6.5 149.8 %all-gather.3.cloned.1.call-start = ((), (), s32[]{:S(2)}) async-start(), calls=%async_computation.3 | async-start | bytes 1081344 | tf_op jit(solution)/shard_map/all_gather | solution.py:79
  8.1 288.6 %all-gather.5.cloned.1.call-start = ((), (), s32[]{:S(2)}) async-start(), calls=%async_computation.4 | async-start | bytes 1081344 | tf_op jit(solution)/shard_map/all_gather | solution.py:80
  296.7 5.5 copy-start.2
  304.3 9.9 %all-to-all-start = ((bf16[4,32,256]{2,1,0:T(8,128)(2,1)}), bf16[4,32,256]{2,1,0:T(8,128)(2,1)S(1)}, u32[]{:S(2)}, u32[]{:S(2)}) async-start(bf16[4,32,256]{2,1,0:T(8,128)(2,1)} %bitcast.5), calls=%async_computation | async-start | bytes 131072 | tf_op jit(solution)/shard_map/all_to_all | solution.py:116
  541.9 4.4 copy-start.1
  541.9 4.4 copy-start.4
  555.4 16.3 %copy-start.3 = (f32[32,8]{0,1:T(8,128)S(1)}, f32[32,8]{0,1:T(8,128)}, u32[]{:S(2)}) copy-start(f32[32,8]{0,1:T(8,128)} %param.20) | copy-start | bytes 3076
  557.7 69.1 %all-to-all-start.2 = ((bf16[128,4,1024]{2,1,0:T(4,128)(2,1)}), bf16[128,4,1024]{2,1,0:T(4,128)(2,1)}, u32[]{:S(2)}, u32[]{:S(2)}) async-start(bf16[128,4,1024]{2,1,0:T(4,128)(2,1)} %reshape.162), calls=%async_computation.2 | async-start | bytes 2097152 | tf_op jit(solution)/shard_map/all_to_all | solution.py:147
Sparse Core Ops, SparseCore 0:
  10.5 145.8 all-gather.2
  159.4 137.1 all-gather.4
where the time goes:
time: 639 us; the launch traced here: 637 us
  waiting for transfers between devices  344 us (54%)
  blocking collectives  218 us (34%)
  local copies, waits for them, and re-layouts  24.7 us (4%)
  starting transfers between devices  18.3 us (3%)
  between operations  13.6 us (2%)
  matrix products  13.4 us (2%)
    all_to_all x1, blocking collectives, body(): lax.all_to_all(outgoing, ('cp', 'dp'), split_axis=0, concat_axis=0, tiled...  198 us
    all_gather x1, waiting for transfers between devices, body(): lax.all_gather(k_mine, 'cp', axis=0, tiled=True)  144 us
    all_gather x1, waiting for transfers between devices, body(): lax.all_gather(v_mine, 'cp', axis=0, tiled=True)  140 us
    all_to_all x1, waiting for transfers between devices, body(): lax.all_to_all(produced.reshape(expert_count, capacity, down_rows.shape[1...  54.9 us
    all_to_all x1, starting transfers between devices, body(): lax.all_to_all(produced.reshape(expert_count, capacity, down_rows.shape[1...  13.9 us
  transfers between devices with their start and end apart: 4, of which 4 were waited for; matrix products, arithmetic and copies ran while one was open for 1% of the time, Pallas kernels for 0%

commit v1 on v0

v1 whole, which is shorter than its diff:
```python
import jax
import jax.numpy as jnp
from jax import lax
from jax.sharding import Mesh, PartitionSpec as P

QUERY_HEADS = 32
KEY_VALUE_HEADS = 2
HEAD_WIDTH = 128
CAP = 4
WINDOW = 17

epsilon = 1e-06
masked_score = -1e30


def attend(q_proj, key_projection, value_projection, segments):
    rows = q_proj.shape[0]
    heads = q_proj.shape[1] // HEAD_WIDTH
    context = lax.axis_index("z") * lax.axis_size("xh") + lax.axis_index("xh")
    blocks = lax.axis_size("z") * lax.axis_size("xh")
    kv_head = lax.axis_index("xl")
    k_mine = lax.dynamic_slice_in_dim(key_projection, kv_head * HEAD_WIDTH, HEAD_WIDTH, 1)
    v_mine = lax.dynamic_slice_in_dim(value_projection, kv_head * HEAD_WIDTH, HEAD_WIDTH, 1)
    kv = lax.all_gather(jnp.concatenate([k_mine, v_mine], 1), ("z", "xh"), axis=0, tiled=True)
    window = min(WINDOW, blocks) * rows
    first_key = jnp.maximum(context + 1 - WINDOW, 0) * rows
    kv = lax.dynamic_slice_in_dim(kv, first_key, window, 0)
    k_all, v_all = kv[:, :HEAD_WIDTH], kv[:, HEAD_WIDTH:]
    seg_keys = lax.dynamic_slice_in_dim(segments, first_key, window, 0)
    first_row = context * rows
    seg_rows = lax.dynamic_slice_in_dim(segments, first_row, rows, 0)
    q_positions = first_row + jnp.arange(rows, dtype=jnp.int32)
    k_positions = first_key + jnp.arange(window, dtype=jnp.int32)
    allowed = (k_positions[None, :] <= q_positions[:, None]) & (
        seg_keys[None, :] == seg_rows[:, None]
    )
    q_heads = q_proj.reshape(rows, heads, HEAD_WIDTH)
    scores = jnp.einsum("rhd,kd->hrk", q_heads, k_all, preferred_element_type=jnp.float32)
    scores = jnp.where(allowed[None], scores * HEAD_WIDTH ** (-0.5), masked_score)
    weights = jnp.exp(scores - jnp.max(scores, 2, keepdims=True))
    total = jnp.sum(weights, 2)
    mixed = jnp.einsum(
        "hrk,kd->hrd", weights.astype(jnp.bfloat16), v_all, preferred_element_type=jnp.float32
    )
    return (mixed / total[:, :, None]).transpose(1, 0, 2).reshape(rows, heads * HEAD_WIDTH)


def body(
    q_proj,
    key_projection,
    value_projection,
    segments,
    resid,
    norm_gain,
    route_ids,
    route_gates,
    w_gate,
    w_up,
    w_down,
):
    n_z, n_xh, n_dp = lax.axis_size("z"), lax.axis_size("xh"), lax.axis_size("dp")
    n_tensor = lax.axis_size("xl") * lax.axis_size("core")
    tensor_index = lax.axis_index("xl") * lax.axis_size("core") + lax.axis_index("core")
    attended = attend(q_proj, key_projection, value_projection, segments)
    after_attn = (resid.astype(jnp.float32) + attended).astype(jnp.bfloat16)
    folded = lax.all_to_all(after_attn, "dp", split_axis=0, concat_axis=1, tiled=True)
    rows, width = folded.shape
    values = folded.astype(jnp.float32)
    squares = lax.psum(jnp.sum(values * values, 1), ("xl", "core"))
    inverse = lax.rsqrt(squares / (width * n_tensor) + epsilon)[:, None]
    gain_here = lax.dynamic_slice_in_dim(norm_gain, tensor_index * width, width, 0)
    normed = (values * inverse * gain_here.astype(jnp.float32)).astype(jnp.bfloat16)

    plane = n_xh * n_dp
    ids = lax.all_gather(route_ids, "z", axis=0)
    gates = lax.all_gather(route_gates, "z", axis=0)
    first_expert = lax.axis_index("z") * plane
    local = first_expert + jnp.arange(plane, dtype=jnp.int32)
    member = ids[:, None, :, :] == local[None, :, None, None]
    named = jnp.any(member, 3)
    weight = jnp.sum(jnp.where(member, gates[:, None], 0.0), 3)
    rank = jnp.cumsum(named.astype(jnp.int32), 2) - 1
    slots = jnp.arange(CAP, dtype=jnp.int32)
    chosen = named[:, :, None, :] & (rank[:, :, None, :] == slots[None, None, :, None])
    picker = chosen.astype(jnp.bfloat16).reshape(n_z, plane * CAP, rows)
    mixer = jnp.where(chosen, weight[:, :, None, :], 0.0).reshape(n_z, plane * CAP, rows)

    tokens = lax.all_gather(normed, "z", axis=0)
    outgoing = jnp.einsum("zsr,zrd->zsd", picker, tokens, preferred_element_type=jnp.float32)
    outgoing = outgoing.astype(jnp.bfloat16).reshape(n_z, plane, CAP, width)
    outgoing = outgoing.transpose(1, 0, 2, 3).reshape(plane, n_z * CAP, width)
    arrived = lax.all_to_all(outgoing, ("xh", "dp"), split_axis=0, concat_axis=0, tiled=True)
    arrived = arrived.reshape(plane * n_z * CAP, width)
    full = lax.all_gather(arrived, ("xl", "core"), axis=1, tiled=True)
    contract = (((1,), (1,)), ((), ()))
    gate_val = lax.dot_general(full, w_gate[0], contract, preferred_element_type=jnp.float32)
    up_val = lax.dot_general(full, w_up[0], contract, preferred_element_type=jnp.float32)
    hidden = (jax.nn.silu(gate_val) * up_val).astype(jnp.bfloat16)
    hidden = lax.all_gather(hidden, ("xl", "core"), axis=1, tiled=True)
    produced = jnp.dot(hidden, w_down[0], preferred_element_type=jnp.float32).astype(jnp.bfloat16)
    returned = lax.all_to_all(
        produced.reshape(plane, n_z * CAP, width), ("xh", "dp"), split_axis=0, concat_axis=0, tiled=True
    )
    returned = returned.reshape(plane, n_z, CAP, width).transpose(1, 0, 2, 3)
    returned = returned.reshape(n_z, plane * CAP, width)
    partial = jnp.einsum(
        "zsr,zsd->zrd",
        mixer,
        returned.astype(jnp.float32),
        precision=lax.Precision.HIGHEST,
        preferred_element_type=jnp.float32,
    )
    expert_sum = lax.psum_scatter(partial, "z", scatter_dimension=0, tiled=False)
    return (values + expert_sum).astype(jnp.bfloat16)


def solution(mesh):
    n_cp, n_tp, n_dp = (mesh.shape[a] for a in ("cp", "tp", "dp"))
    fine = Mesh(
        mesh.devices.reshape(n_cp // 2, 2, n_tp // 2, 2, n_dp), ("z", "xh", "xl", "core", "dp")
    )
    cp, tp = ("z", "xh"), ("xl", "core")
    placed = (
        P(cp, tp + ("dp",)),
        P(cp, None),
        P(cp, None),
        P(),
        P(cp, tp + ("dp",)),
        P(),
        P(cp + ("dp",), None),
        P(cp + ("dp",), None),
        P(cp + ("dp",), tp, None),
        P(cp + ("dp",), tp, None),
        P(cp + ("dp",), None, tp),
    )
    return jax.shard_map(
        body, mesh=fine, in_specs=placed, out_specs=P(cp + ("dp",), tp), check_vma=False
    )
```

time: 639 us -> 450 us (0.70)
  blocking collectives: 218 us -> 108 us
  waiting for transfers between devices: 344 us -> 287 us
  starting transfers between devices: 18.3 us -> 4.37 us
  local copies, waits for them, and re-layouts: 24.7 us -> 11.6 us
    all_to_all x1 -> x2, blocking collectives: 198 us -> 38.8 us  [the longest x1 21.8 us: body(): lax.all_to_all(produced.reshape(plane, n_z * CAP, width), ('xh', 'dp'), s...]
    all_gather x2 -> x3, waiting for transfers between devices: 284 us -> 208 us  [the longest x1 152 us: attend(): lax.all_gather(jnp.concatenate([k_mine, v_mine], 1), ('z', 'xh'), axis=0,...]
    reduce_scatter x0 -> x1, waiting for transfers between devices: none -> 73.6 us  [body(): lax.psum_scatter(partial, 'z', scatter_dimension=0, tiled=False)]
    all_to_all x1 -> x0, waiting for transfers between devices: 54.9 us -> none  [body(): lax.all_to_all(produced.reshape(expert_count, capacity, down_rows.shape[1...]
    all_gather x2 -> x3, blocking collectives: 13.4 us -> 63.7 us  [the longest x1 28.2 us: body(): ids = lax.all_gather(route_ids, 'z', axis=0)]
    all_to_all x1 -> x0, starting transfers between devices: 13.9 us -> none  [body(): lax.all_to_all(produced.reshape(expert_count, capacity, down_rows.shape[1...]
    reshape x5 -> x7, local copies, waits for them, and re-layouts: 16.8 us -> 8.8 us  [the longest x2 3.96 us: body(): returned = returned.reshape(plane, n_z, CAP, width).transpose(1, 0, 2, 3)]
    dot_general x6 -> x7, matrix products: 12.6 us -> 15.6 us  [the longest x1 4.35 us: body(): lax.dot_general(full, w_gate[0], contract, preferred_element_type=jnp.flo...]
  transfers between devices with their start and end apart: 4 -> 5, of which waited for: 4 -> 5; matrix products, arithmetic and copies ran while one was open for 1% -> 2% of each run, Pallas kernels for 0% -> 0%
where the time goes in v1:
time: 450 us
  waiting for transfers between devices  287 us (64%)
  blocking collectives  108 us (24%)
  matrix products  15.6 us (3%)
  between operations  13.4 us (3%)
  local copies, waits for them, and re-layouts  11.6 us (3%)
  other arithmetic  9.66 us (2%)
    all_gather x1, waiting for transfers between devices, attend(): lax.all_gather(jnp.concatenate([k_mine, v_mine], 1), ('z', 'xh'), axis=0,...  152 us
    reduce_scatter x1, waiting for transfers between devices, body(): lax.psum_scatter(partial, 'z', scatter_dimension=0, tiled=False)  73.6 us
    all_gather x1, waiting for transfers between devices, body(): full = lax.all_gather(arrived, ('xl', 'core'), axis=1, tiled=True)  48.6 us
    all_gather x1, blocking collectives, body(): ids = lax.all_gather(route_ids, 'z', axis=0)  28.2 us
    all_gather x1, blocking collectives, body(): gates = lax.all_gather(route_gates, 'z', axis=0)  26.4 us
    all_to_all x1, blocking collectives, body(): lax.all_to_all(produced.reshape(plane, n_z * CAP, width), ('xh', 'dp'), s...  21.8 us
    all_to_all x1, blocking collectives, body(): lax.all_to_all(outgoing, ('xh', 'dp'), split_axis=0, concat_axis=0, tiled...  17 us
    all_gather x1, blocking collectives, body(): hidden = lax.all_gather(hidden, ('xl', 'core'), axis=1, tiled=True)  9.17 us
  transfers between devices with their start and end apart: 5, of which 5 were waited for; matrix products, arithmetic and copies ran while one was open for 2% of the time, Pallas kernels for 0%

profile of v1, /device:TPU:6, one launch (start us, length us, event | category | flops | bytes accessed | tf_op | source)
XLA Modules:
  0.0 449.7 jit_solution(16391398025174104697)
XLA Ops:
  6.5 0.9 constant_dynamic-slice_fusion
  8.1 0.8 dynamic_slice.19
  8.9 0.8 dynamic_slice.18
  9.7 1.4 compare_and_fusion
  11.1 152.5 %all-gather.8.cloned.1.call-done = bf16[4096,256]{1,0:T(8,128)(2,1)} async-done(((bf16[128,256]{1,0:T(8,128)(2,1)}), bf16[4096,256]{1,0:T(8,128)(2,1)}) %all-gather.8.cloned.1.call-update) | async-done | bytes 2097168 | tf_op jit(solution)/shard_map/all_gather | solution.py:24
  163.6 1.6 fusion.33
  165.5 1.6 fusion.19
  167.9 4.3 all-to-all-start
  172.2 0.7 dynamic-slice_convert_fusion
  172.8 4.9 %all-to-all-done = bf16[4,32,256]{2,1,0:T(8,128)(2,1)S(1)} async-done(((bf16[4,32,256]{2,1,0:T(8,128)(2,1)}), bf16[4,32,256]{2,1,0:T(8,128)(2,1)S(1)}, u32[]{:S(2)}, u32[]{:S(2)}) %all-to-all-start) | async-done | bytes 65568 | tf_op jit(solution)/shard_map/all_to_all | solution.py:66
  177.9 5.8 %psum.7 = f32[32]{0:T(128)S(1)} all-reduce(f32[32]{0:T(128)S(1)} %fusion.27), channel_id=1, replica_groups=mesh['z'=16,'xh'=2,'xl'=2,'core'=2,'dp'=4] {'xl','core'}, use_global_device_ids=true, to_apply=%region_6.7 | all-reduce | flops 32 | bytes 256 | tf_op jit(solution)/shard_map/psum | solution.py:69
  183.9 0.7 multiply_convert_fusion
  184.7 28.2 %all-gather.2 = s32[16,32,8]{1,2,0:T(8,128)S(1)} all-gather(s32[1,32,8]{1,2,0:T(8,128)S(1)} %bitcast.84), channel_id=2, replica_groups=mesh['z'=16,'xh'=2,'xl'=2,'core'=2,'dp'=4] {'z'}, dimensions={0}, use_global_device_ids=true | all-gather | bytes 17408 | tf_op jit(solution)/shard_map/all_gather | solution.py:75
  213.2 3.0 reduce_window_sum.11
  216.2 26.4 %all-gather.3 = f32[16,32,8]{1,2,0:T(8,128)S(1)} all-gather(f32[1,32,8]{1,2,0:T(8,128)S(1)} %bitcast.85), channel_id=3, replica_groups=mesh['z'=16,'xh'=2,'xl'=2,'core'=2,'dp'=4] {'z'}, dimensions={0}, use_global_device_ids=true | all-gather | bytes 17408 | tf_op jit(solution)/shard_map/all_gather | solution.py:76
  243.0 7.1 %all-gather.10.cloned.1.call-done = bf16[16,32,1024]{2,1,0:T(8,128)(2,1)} async-done(((bf16[1,32,1024]{2,1,0:T(8,128)(2,1)}), bf16[16,32,1024]{2,1,0:T(8,128)(2,1)}) %all-gather.10.cloned.1.call-update) | async-done | bytes 1048592 | tf_op jit(solution)/shard_map/all_gather | solution.py:88
  250.1 1.6 convolution_convert_fusion
  251.7 1.2 reshape.183
  252.9 1.6 copy.89
  255.1 17.0 %all_to_all.23 = bf16[8,64,1024]{2,1,0:T(8,128)(2,1)} all-to-all(bf16[8,64,1024]{2,1,0:T(8,128)(2,1)S(1)} %copy.90), channel_id=1, replica_groups=mesh['z'=16,'xh'=2,'xl'=2,'core'=2,'dp'=4] {'xh','dp'}, dimensions={0} | all-to-all | bytes 2097152 | tf_op jit(solution)/shard_map/all_to_all | solution.py:92
  272.2 48.6 %all-gather.12.cloned.1.call-done = bf16[512,4096]{1,0:T(8,128)(2,1)} async-done(((bf16[512,1024]{1,0:T(8,128)(2,1)}), bf16[512,4096]{1,0:T(8,128)(2,1)}) %all-gather.12.cloned.1.call-update) | async-done | bytes 4194320 | tf_op jit(solution)/shard_map/all_gather | solution.py:94
  320.9 4.3 fusion.8
  325.2 3.0 fusion.16
  328.3 9.2 %all_gather.32 = bf16[512,768]{0,1:T(8,128)(2,1)S(1)} all-gather(bf16[512,192]{0,1:T(8,128)(2,1)S(1)} %fusion.16), channel_id=1, replica_groups=mesh['z'=16,'xh'=2,'xl'=2,'core'=2,'dp'=4] {'xl','core'}, dimensions={1}, use_global_device_ids=true | all-gather | bytes 983040 | tf_op jit(solution)/shard_map/all_gather | solution.py:99
  337.5 1.0 fusion.10
  338.5 21.8 %all_to_all.24 = bf16[8,64,1024]{2,1,0:T(8,128)(2,1)S(1)} all-to-all(bf16[8,64,1024]{2,1,0:T(8,128)(2,1)S(1)} %bitcast.80), channel_id=1, replica_groups=mesh['z'=16,'xh'=2,'xl'=2,'core'=2,'dp'=4] {'xh','dp'}, dimensions={0} | all-to-all | bytes 2097152 | tf_op jit(solution)/shard_map/all_to_all | solution.py:101
  360.3 1.2 reshape.187
  361.5 2.7 copy.109
  364.2 1.3 reshape.188
  365.6 2.4 fusion.23
  368.0 73.6 %reduce-scatter.2.cloned.1.call-done = f32[1,32,1024]{2,1,0:T(8,128)} async-done(((f32[16,32,1024]{2,1,0:T(8,128)}), f32[1,32,1024]{2,1,0:T(8,128)}) %reduce-scatter.2.cloned.1.call-update) | async-done | bytes 131088 | tf_op jit(solution)/shard_map/reduce_scatter | solution.py:113
  441.6 1.5 fusion.28
  (42 shorter events, 3.5 us)
Async XLA Ops:
  6.5 330.9 %copy-start = (bf16[1,768,1024]{2,1,0:T(8,128)(2,1)S(1)}, bf16[1,768,1024]{2,1,0:T(8,128)(2,1)}, u32[]{:S(2)}) copy-start(bf16[1,768,1024]{2,1,0:T(8,128)(2,1)} %param.21) | copy-start | bytes 4718596
  6.5 157.0 %all-gather.8.cloned.1.call-start = ((), (), s32[]{:S(2)}) async-start(), calls=%async_computation.4 | async-start | bytes 2162688 | tf_op jit(solution)/shard_map/all_gather | solution.py:24
  165.5 1.8 copy-start.1
  165.5 19.2 %copy-start.2 = (s32[32,8]{0,1:T(8,128)S(1)}, s32[32,8]{0,1:T(8,128)}, u32[]{:S(2)}) copy-start(s32[32,8]{0,1:T(8,128)} %param.17) | copy-start | bytes 3076
  165.5 50.7 %copy-start.3 = (f32[32,8]{0,1:T(8,128)S(1)}, f32[32,8]{0,1:T(8,128)}, u32[]{:S(2)}) copy-start(f32[32,8]{0,1:T(8,128)} %param.18) | copy-start | bytes 3076
  167.9 9.9 %all-to-all-start = ((bf16[4,32,256]{2,1,0:T(8,128)(2,1)}), bf16[4,32,256]{2,1,0:T(8,128)(2,1)S(1)}, u32[]{:S(2)}, u32[]{:S(2)}) async-start(bf16[4,32,256]{2,1,0:T(8,128)(2,1)} %bitcast.6), calls=%async_computation | async-start | bytes 131072 | tf_op jit(solution)/shard_map/all_to_all | solution.py:66
  172.2 77.9 %all-gather.10.cloned.1.call-start = ((), (), s32[]{:S(2)}) async-start(), calls=%async_computation.5 | async-start | bytes 1114112 | tf_op jit(solution)/shard_map/all_gather | solution.py:88
  184.6 136.3 %all-gather.12.cloned.1.call-start = ((), (), s32[]{:S(2)}) async-start(), calls=%async_computation.6 | async-start | bytes 5242880 | tf_op jit(solution)/shard_map/all_gather | solution.py:94
  272.2 169.4 %reduce-scatter.2.cloned.1.call-start = ((), (), s32[]{:S(2)}) async-start(), calls=%async_computation.7 | async-start | bytes 2228224 | tf_op jit(solution)/shard_map/reduce_scatter | solution.py:113
  320.9 4.4 copy-start.4
Sparse Core Ops, SparseCore 0:
  10.5 153.0 all-gather.7
  184.7 65.2 all-gather.9
  272.3 48.5 all-gather.11
  368.1 73.4 reduce-scatter.1

commit v2 on v1

v2 whole, which is shorter than its diff:
```python
import functools

import jax
import jax.numpy as jnp
from jax import lax
from jax.experimental import pallas as pl
from jax.experimental.pallas import tpu as pltpu
from jax.sharding import Mesh, PartitionSpec as P

HEAD_WIDTH = 128
CAP = 4
REACH = 2048
BLOCK = 32
GROUP = 4
SLOTS = GROUP * CAP
SPLIT = 2

epsilon = 1e-06
masked_score = -1e30
bf16, f32 = jnp.bfloat16, jnp.float32
MESH = pl.DeviceIdType.MESH


def sizes():
    return {a: lax.axis_size(a) for a in ("z", "xh", "xl", "core", "dp")}


def places():
    return {a: lax.axis_index(a) for a in ("z", "xh", "xl", "core", "dp")}


def moved(me, n, **steps):
    return {a: lax.rem(me[a] + n[a] + s, n[a]) for a, s in steps.items()}


def shifts(n, axes):
    found = [{}]
    for a in axes:
        found = [{**f, a: s} for f in found for s in range(n[a])]
    return found[1:]


def copy_to(src, dst, send, recv, device):
    return pltpu.make_async_remote_copy(
        src_ref=src, dst_ref=dst, send_sem=send, recv_sem=recv, device_id=device, device_id_type=MESH
    )


def greet(me, n, steps):
    barrier = pltpu.get_barrier_semaphore()
    for s in steps:
        pl.semaphore_signal(barrier, inc=1, device_id=moved(me, n, **s), device_id_type=MESH)
    pl.semaphore_wait(barrier, len(steps))


def up_place(k):
    return 2 * k - 1 if k else 0


def attention_kernel(
    n, q_ref, k_ref, v_ref, seg_ref, resid_ref, gain_ref, ids_ref, gates_ref,
    normed_ref, kept_ref, routes_ref,
    kv, queries, table, routes, stage, fold,
    z_send, z_recv, plane_send, plane_recv, core_send, core_recv,
    route_send, route_recv, fold_send, fold_recv,
):
    me = places()
    rows = q_ref.shape[0]
    heads = q_ref.shape[1] // HEAD_WIDTH
    plane_rows = n["xh"] * rows
    reach = min(-(-REACH // plane_rows), n["z"] - 1)
    up, down = n["z"] // 2, n["z"] // 2 - 1
    plane = shifts(n, ("xh", "dp"))
    group = shifts(n, ("xl", "core", "dp"))
    line = [{"z": s} for s in range(1, n["z"])]
    greet(me, n, line + plane + [g for g in group if g.get("xl") or g.get("core")])

    core = me["core"]
    quarter = rows // n["dp"]
    start = pl.multiple_of(me["xh"] * rows + me["dp"] * quarter, quarter)
    here = pl.ds(start, quarter)
    head = pl.ds(pl.multiple_of(me["xl"] * HEAD_WIDTH, HEAD_WIDTH), HEAD_WIDTH)
    mine = pl.ds(pl.multiple_of(me["dp"] * quarter, quarter), quarter)
    kv[core, 0, here, :] = jnp.where(core == 0, k_ref[mine, head], v_ref[mine, head])
    z_copies = {
        d: copy_to(
            kv.at[core, 0, here], kv.at[core, d, here], z_send.at[d], z_recv.at[d], moved(me, n, z=d)
        )
        for d in range(1, reach + 1)
    }
    for c in z_copies.values():
        c.start()

    def plane_copy(d, i):
        return copy_to(
            kv.at[core, d, here], kv.at[core, d, here],
            plane_send.at[d, i], plane_recv.at[d, i], moved(me, n, **plane[i]),
        )

    def core_copy(d):
        return copy_to(
            kv.at[core, d], kv.at[core, d], core_send.at[d], core_recv.at[d], moved(me, n, core=1)
        )

    for i in range(len(plane)):
        plane_copy(0, i).start()

    lanes = ids_ref.shape[1]
    experts = table.shape[1]
    per_plane = experts // n["z"]
    expert = lax.broadcasted_iota(jnp.int32, (experts, lanes), 0)
    named = jnp.zeros((experts, lanes), f32)
    weight = jnp.zeros((experts, lanes), f32)
    for j in range(ids_ref.shape[0]):
        equal = expert == ids_ref[j : j + 1, :]
        named += jnp.where(equal, 1.0, 0.0)
        weight += jnp.where(equal, gates_ref[j : j + 1, :], 0.0)
    earlier = lax.broadcasted_iota(jnp.int32, (lanes, lanes), 0)
    later = lax.broadcasted_iota(jnp.int32, (lanes, lanes), 1)
    before = (earlier < later) & (earlier // BLOCK == later // BLOCK)
    rank = jnp.dot(
        named.astype(bf16), jnp.where(before, 1.0, 0.0).astype(bf16), preferred_element_type=f32
    )
    table[0] = jnp.where(named > 0.5, rank, 2.0 * CAP)
    table[1] = weight

    def rows_of(plane_index):
        return pl.ds(pl.multiple_of(plane_index * per_plane, per_plane), per_plane)

    route_copies = []
    for k, place in [(k, 2 * k - 1) for k in range(1, up + 1)] + [(-k, 2 * k) for k in range(1, down + 1)]:
        target = moved(me, n, z=k)
        route_copies.append(
            copy_to(
                table.at[:, rows_of(target["z"])], routes.at[place],
                route_send.at[place], route_recv.at[place], target,
            )
        )
        route_copies[-1].start()
    routes[0] = table[:, rows_of(me["z"]), :]

    for h in range(heads):
        queries[h * rows : (h + 1) * rows] = q_ref[:, h * HEAD_WIDTH : (h + 1) * HEAD_WIDTH]
    all_rows = heads * rows
    context = me["z"] * n["xh"] + me["xh"]
    first_row = pl.multiple_of(context * rows, rows)
    seg_here = seg_ref[:, pl.ds(first_row, rows)].astype(f32)
    r = lax.broadcasted_iota(jnp.int32, (all_rows, rows), 0)
    c = lax.broadcasted_iota(jnp.int32, (all_rows, rows), 1)
    seg_rows = jnp.sum(jnp.where(lax.rem(r, rows) == c, seg_here, 0.0), 1, keepdims=True)
    q_position = first_row + lax.rem(
        lax.broadcasted_iota(jnp.int32, (all_rows, plane_rows), 0), rows
    )
    k_offset = lax.broadcasted_iota(jnp.int32, (all_rows, plane_rows), 1)
    state = None
    for t in range(reach + 3):
        if 1 <= t <= reach:
            z_copies[t].wait_recv()
            for i in range(len(plane)):
                plane_copy(t, i).start()
        if 0 <= t - 1 <= reach:
            for i in range(len(plane)):
                plane_copy(t - 1, i).wait_recv()
            core_copy(t - 1).start()
        d = t - 2
        if d < 0:
            continue
        core_copy_back = copy_to(
            kv.at[1 - core, d], kv.at[1 - core, d], core_send.at[d], core_recv.at[d], moved(me, n, core=1)
        )
        core_copy_back.wait_recv()
        first_key = pl.multiple_of(lax.rem(me["z"] + n["z"] - d, n["z"]) * plane_rows, plane_rows)
        scores = (
            lax.dot_general(
                queries[...], kv[0, d], (((1,), (1,)), ((), ())), preferred_element_type=f32
            )
            * HEAD_WIDTH ** (-0.5)
        )
        seg_keys = seg_ref[:, pl.ds(first_key, plane_rows)].astype(f32)
        allowed = (first_key + k_offset <= q_position) & (seg_keys == seg_rows)
        scores = jnp.where(allowed, scores, masked_score)
        top = jnp.max(scores, 1, keepdims=True)
        if state is None:
            weights = jnp.exp(scores - top)
            total = jnp.sum(weights, 1, keepdims=True)
            acc = jnp.dot(weights.astype(bf16), kv[1, d], preferred_element_type=f32)
        else:
            old_top, old_total, old_acc = state
            top = jnp.maximum(old_top, top)
            weights = jnp.exp(scores - top)
            fade = jnp.exp(old_top - top)
            total = old_total * fade + jnp.sum(weights, 1, keepdims=True)
            acc = old_acc * fade + jnp.dot(
                weights.astype(bf16), kv[1, d], preferred_element_type=f32
            )
        state = (top, total, acc)
    attended = state[2] / state[1]
    for h in range(heads):
        cols = slice(h * HEAD_WIDTH, (h + 1) * HEAD_WIDTH)
        stage[:, cols] = (
            resid_ref[:, cols].astype(f32) + attended[h * rows : (h + 1) * rows]
        ).astype(bf16)

    tensor = me["xl"] * n["core"] + core
    slab = tensor * n["dp"] + me["dp"]

    def rows_for(y):
        return pl.ds(pl.multiple_of(y * quarter, quarter), quarter)

    fold_copies = []
    for i, g in enumerate(group):
        target = moved(me, n, **g)
        fold_copies.append(
            copy_to(
                stage.at[rows_for(target["dp"])], fold.at[slab],
                fold_send.at[i], fold_recv.at[i], target,
            )
        )
        fold_copies[-1].start()
    fold[slab] = stage[rows_for(me["dp"]), :]
    for i in range(len(line)):
        route_copies[i].wait_recv()
    routes_ref[...] = routes[...]
    for f in fold_copies:
        f.wait_recv()
    slabs = fold.shape[0]
    width = stage.shape[1]
    squares = jnp.zeros((quarter, width), f32)
    for s in range(slabs):
        v = fold[s].astype(f32)
        squares += v * v
    squares = jnp.sum(squares, 1, keepdims=True)
    inverse = lax.rsqrt(squares / (slabs * width) + epsilon)
    per_core = slabs // n["core"]
    for i in range(per_core):
        s = core * per_core + i
        gain = gain_ref[:, pl.ds(pl.multiple_of(s * width, width), width)].astype(f32)
        normed_ref[:, i * width : (i + 1) * width] = (
            fold[s].astype(f32) * inverse * gain
        ).astype(bf16)
    for i in range(n["dp"]):
        kept_ref[:, i * width : (i + 1) * width] = fold[tensor * n["dp"] + i]

    for c in z_copies.values():
        c.wait_send()
    for d in range(reach + 1):
        for i in range(len(plane)):
            plane_copy(d, i).wait_send()
        core_copy(d).wait_send()
    for c in route_copies + fold_copies:
        c.wait_send()


def attention_call(q, k, v, segments, resid, gain, ids, gates):
    n = sizes()
    rows, width = q.shape
    plane_rows = n["xh"] * rows
    reach = min(-(-REACH // plane_rows), n["z"] - 1)
    per_plane = n["xh"] * n["dp"]
    experts = per_plane * n["z"]
    lanes = ids.shape[1]
    quarter = rows // n["dp"]
    slabs = n["xl"] * n["core"] * n["dp"]
    dma = pltpu.SemaphoreType.DMA
    return pl.pallas_call(
        functools.partial(attention_kernel, n),
        out_shape=(
            jax.ShapeDtypeStruct((quarter, slabs * width // n["core"]), bf16),
            jax.ShapeDtypeStruct((quarter, n["dp"] * width), bf16),
            jax.ShapeDtypeStruct((n["z"], 2, per_plane, lanes), f32),
        ),
        in_specs=[pl.BlockSpec(memory_space=pltpu.VMEM)] * 8,
        out_specs=(pl.BlockSpec(memory_space=pltpu.VMEM),) * 3,
        scratch_shapes=[
            pltpu.VMEM((2, reach + 1, plane_rows, HEAD_WIDTH), bf16),
            pltpu.VMEM((rows * width // HEAD_WIDTH, HEAD_WIDTH), bf16),
            pltpu.VMEM((2, experts, lanes), f32),
            pltpu.VMEM((n["z"], 2, per_plane, lanes), f32),
            pltpu.VMEM((rows, width), bf16),
            pltpu.VMEM((slabs, quarter, width), bf16),
            dma((reach + 1,)),
            dma((reach + 1,)),
            dma((reach + 1, per_plane)),
            dma((reach + 1, per_plane)),
            dma((reach + 1,)),
            dma((reach + 1,)),
            dma((n["z"],)),
            dma((n["z"],)),
            dma((slabs,)),
            dma((slabs,)),
        ],
        compiler_params=pltpu.CompilerParams(
            collective_id=0, has_side_effects=True, vmem_limit_bytes=32 * 1024 * 1024
        ),
        name="attention",
    )(q, k, v, segments, resid, gain, ids, gates)


def expert_kernel(
    n, normed_ref, kept_ref, routes_ref, gate_hbm, up_hbm, down_hbm,
    mixed_ref,
    w_gate, w_up, w_down, tokens, picked, arrived, hidden, produced, returned, partial,
    fall_out, fall_in, rise_out, rise_in,
    w_sem, up_send, up_recv, down_send, down_recv, pick_send, pick_recv, core_send, core_recv,
    hid_send, hid_recv, ret_send, ret_recv, fall_send, fall_recv, rise_send, rise_recv,
):
    me = places()
    up, down = n["z"] // 2, n["z"] // 2 - 1
    groups = n["z"] // GROUP
    plane = shifts(n, ("xh", "dp"))
    tensor_steps = shifts(n, ("xl", "core"))
    experts = n["xh"] * n["dp"]
    core = me["core"]
    tensor = me["xl"] * n["core"] + core
    mine = me["xh"] * n["dp"] + me["dp"]
    w_copies = [
        pltpu.make_async_copy(a, b, w_sem.at[i])
        for i, (a, b) in enumerate(((gate_hbm, w_gate), (up_hbm, w_up), (down_hbm, w_down)))
    ]
    for c in w_copies:
        c.start()
    tokens[0] = normed_ref[...]
    greet(me, n, [{"z": 1}, {"z": -1}] + plane + tensor_steps)

    def up_copy(k):
        return copy_to(
            tokens.at[up_place(k)], tokens.at[up_place(k + 1)],
            up_send.at[k], up_recv.at[k], moved(me, n, z=1),
        )

    def down_copy(k):
        return copy_to(
            tokens.at[2 * k], tokens.at[2 * k + 2],
            down_send.at[k], down_recv.at[k], moved(me, n, z=-1),
        )

    def pick_copy(g, i):
        to = moved(me, n, **plane[i])
        to_index = to.get("xh", me["xh"]) * n["dp"] + to.get("dp", me["dp"])
        return copy_to(
            picked.at[g, to_index], arrived.at[core, g, mine],
            pick_send.at[g, i], pick_recv.at[g, i], to,
        )

    def core_copy(g, half):
        return copy_to(
            arrived.at[half, g], arrived.at[half, g],
            core_send.at[g], core_recv.at[g], moved(me, n, core=1),
        )

    def hid_copy(g, i):
        return copy_to(
            hidden.at[g, tensor], hidden.at[g, tensor],
            hid_send.at[g, i], hid_recv.at[g, i], moved(me, n, **tensor_steps[i]),
        )

    def ret_copy(g, i):
        back = {a: -s for a, s in plane[i].items()}
        to = moved(me, n, **back)
        to_index = to.get("xh", me["xh"]) * n["dp"] + to.get("dp", me["dp"])
        return copy_to(
            produced.at[g, to_index], returned.at[g, mine],
            ret_send.at[g, i], ret_recv.at[g, i], to,
        )

    def slots_of(g):
        lanes = routes_ref.shape[-1]
        lane = lax.broadcasted_iota(jnp.int32, (experts, lanes), 1)
        rank, weight = routes_ref[GROUP * g, 0], routes_ref[GROUP * g, 1]
        for j in range(1, GROUP):
            own = lane // BLOCK == j
            rank = jnp.where(own, routes_ref[GROUP * g + j, 0], rank)
            weight = jnp.where(own, routes_ref[GROUP * g + j, 1], weight)
        shape = (experts, SLOTS, lanes)
        slot = lax.broadcasted_iota(jnp.int32, shape, 1)
        token = lax.broadcasted_iota(jnp.int32, shape, 2)
        held = (jnp.broadcast_to(rank[:, None, :], shape) == lax.rem(slot, CAP).astype(f32)) & (
            token // BLOCK == slot // CAP
        )
        weight = jnp.where(held, jnp.broadcast_to(weight[:, None, :], shape), 0.0)
        flat = (experts * SLOTS, lanes)
        return jnp.where(held, 1.0, 0.0).reshape(flat), weight.reshape(flat)

    def pick(g):
        chosen, _ = slots_of(g)
        block = tokens[GROUP * g : GROUP * (g + 1)].reshape(GROUP * BLOCK, tokens.shape[2])
        out = jnp.dot(chosen.astype(bf16), block, preferred_element_type=f32).astype(bf16)
        picked[g] = out.reshape(picked.shape[1:])
        for i in range(len(plane)):
            pick_copy(g, i).start()
        arrived[core, g, mine] = picked[g, mine]

    def pass_on(g):
        for i in range(len(plane)):
            pick_copy(g, i).wait_recv()
        core_copy(g, core).start()

    contract = (((1,), (1,)), ((), ()))
    n_slots = experts * SLOTS

    def into_hidden(g):
        core_copy(g, 1 - core).wait_recv()
        gate_val = up_val = None
        half = arrived.shape[-1]
        for h in range(n["core"]):
            x = arrived[h, g].reshape(n_slots, half)
            cols = slice(h * half, (h + 1) * half)
            a = lax.dot_general(x, w_gate[0, :, cols], contract, preferred_element_type=f32)
            b = lax.dot_general(x, w_up[0, :, cols], contract, preferred_element_type=f32)
            gate_val = a if gate_val is None else gate_val + a
            up_val = b if up_val is None else up_val + b
        hidden[g, tensor] = (gate_val / (1.0 + jnp.exp(-gate_val)) * up_val).astype(bf16)
        for i in range(len(tensor_steps)):
            hid_copy(g, i).start()

    def out_of_hidden(g):
        for i in range(len(tensor_steps)):
            hid_copy(g, i).wait_recv()
        units = hidden.shape[-1]
        out = None
        for s in range(hidden.shape[1]):
            term = jnp.dot(
                hidden[g, s], w_down[0, s * units : (s + 1) * units, :], preferred_element_type=f32
            )
            out = term if out is None else out + term
        produced[g] = out.astype(bf16).reshape(produced.shape[1:])
        for i in range(len(plane)):
            ret_copy(g, i).start()
        returned[g, mine] = produced[g, mine]

    def mix(g):
        _, weight = slots_of(g)
        for i in range(len(plane)):
            ret_copy(g, i).wait_recv()
        high = weight.astype(bf16)
        low = (weight - high.astype(f32)).astype(bf16)
        back = returned[g].reshape(n_slots, returned.shape[-1])
        over = (((0,), (0,)), ((), ()))
        total = lax.dot_general(high, back, over, preferred_element_type=f32)
        total += lax.dot_general(low, back, over, preferred_element_type=f32)
        partial[GROUP * g : GROUP * (g + 1)] = total.reshape(GROUP, BLOCK, total.shape[-1])

    up_copy(0).start()
    down_copy(0).start()
    for c in w_copies:
        c.wait()
    for step in range(1, up + 1):
        up_copy(step - 1).wait_recv()
        if step < up:
            up_copy(step).start()
        if step <= down:
            down_copy(step - 1).wait_recv()
            if step < down:
                down_copy(step).start()
        if step % 2:
            continue
        g = step // 2 - 1
        pick(g)
        if g >= 1:
            pass_on(g - 1)
        if g >= 2:
            into_hidden(g - 2)
        if g >= 3:
            out_of_hidden(g - 3)
    for g in range(groups, groups + 3):
        if 0 <= g - 1 < groups:
            pass_on(g - 1)
        if 0 <= g - 2 < groups:
            into_hidden(g - 2)
        if 0 <= g - 3 < groups:
            out_of_hidden(g - 3)

    part_width = partial.shape[-1] // SPLIT

    def piece(k_place, s):
        return partial[k_place, :, s * part_width : (s + 1) * part_width]

    def fall_copy(k, s):
        return copy_to(
            fall_out.at[k - 1, s], fall_in.at[k - 1, s],
            fall_send.at[k - 1, s], fall_recv.at[k - 1, s], moved(me, n, z=-1),
        )

    def rise_copy(k, s):
        return copy_to(
            rise_out.at[k - 1, s], rise_in.at[k - 1, s],
            rise_send.at[k - 1, s], rise_recv.at[k - 1, s], moved(me, n, z=1),
        )

    mixed_groups = set()

    def need(place):
        if place // GROUP not in mixed_groups:
            mixed_groups.add(place // GROUP)
            mix(place // GROUP)

    for t in range(up):
        k, j = up - t, down - t
        need(2 * k - 1)
        for s in range(SPLIT):
            total = piece(2 * k - 1, s)
            if t:
                fall_copy(k + 1, s).wait_recv()
                total = total + fall_in[k, s].astype(f32)
            fall_out[k - 1, s] = total.astype(bf16)
            fall_copy(k, s).start()
        if j < 1:
            continue
        need(2 * j)
        for s in range(SPLIT):
            total = piece(2 * j, s)
            if t:
                rise_copy(j + 1, s).wait_recv()
                total = total + rise_in[j, s].astype(f32)
            rise_out[j - 1, s] = total.astype(bf16)
            rise_copy(j, s).start()
    for s in range(SPLIT):
        cols = slice(s * part_width, (s + 1) * part_width)
        total = kept_ref[:, cols].astype(f32) + piece(0, s)
        if down:
            rise_copy(1, s).wait_recv()
            total += rise_in[0, s].astype(f32)
        fall_copy(1, s).wait_recv()
        mixed_ref[:, cols] = (total + fall_in[0, s].astype(f32)).astype(bf16)

    for k in range(up):
        up_copy(k).wait_send()
    for k in range(down):
        down_copy(k).wait_send()
    for g in range(groups):
        core_copy(g, core).wait_send()
        for i in range(len(plane)):
            pick_copy(g, i).wait_send()
            ret_copy(g, i).wait_send()
        for i in range(len(tensor_steps)):
            hid_copy(g, i).wait_send()
    for s in range(SPLIT):
        for k in range(1, up + 1):
            fall_copy(k, s).wait_send()
        for k in range(1, down + 1):
            rise_copy(k, s).wait_send()


def expert_call(normed, kept, routes, w_gate, w_up, w_down):
    n = sizes()
    up, down = n["z"] // 2, n["z"] // 2 - 1
    groups = n["z"] // GROUP
    experts = n["xh"] * n["dp"]
    tensors = n["xl"] * n["core"]
    half, width = normed.shape[1], kept.shape[1]
    units = w_gate.shape[1]
    n_slots = experts * SLOTS
    part_width = width // SPLIT
    dma = pltpu.SemaphoreType.DMA
    vmem = pl.BlockSpec(memory_space=pltpu.VMEM)
    hbm = pl.BlockSpec(memory_space=pl.ANY)
    return pl.pallas_call(
        functools.partial(expert_kernel, n),
        out_shape=jax.ShapeDtypeStruct((BLOCK, width), bf16),
        in_specs=[vmem] * 3 + [hbm] * 3,
        out_specs=vmem,
        scratch_shapes=[
            pltpu.VMEM(w_gate.shape, bf16),
            pltpu.VMEM(w_up.shape, bf16),
            pltpu.VMEM(w_down.shape, bf16),
            pltpu.VMEM((n["z"], BLOCK, half), bf16),
            pltpu.VMEM((groups, experts, SLOTS, half), bf16),
            pltpu.VMEM((n["core"], groups, experts, SLOTS, half), bf16),
            pltpu.VMEM((groups, tensors, n_slots, units), bf16),
            pltpu.VMEM((groups, experts, SLOTS, width), bf16),
            pltpu.VMEM((groups, experts, SLOTS, width), bf16),
            pltpu.VMEM((n["z"], BLOCK, width), f32),
            pltpu.VMEM((up, SPLIT, BLOCK, part_width), bf16),
            pltpu.VMEM((up, SPLIT, BLOCK, part_width), bf16),
            pltpu.VMEM((max(down, 1), SPLIT, BLOCK, part_width), bf16),
            pltpu.VMEM((max(down, 1), SPLIT, BLOCK, part_width), bf16),
            dma((3,)),
            dma((up,)),
            dma((up,)),
            dma((max(down, 1),)),
            dma((max(down, 1),)),
            dma((groups, experts)),
            dma((groups, experts)),
            dma((groups,)),
            dma((groups,)),
            dma((groups, tensors)),
            dma((groups, tensors)),
            dma((groups, experts)),
            dma((groups, experts)),
            dma((up, SPLIT)),
            dma((up, SPLIT)),
            dma((max(down, 1), SPLIT)),
            dma((max(down, 1), SPLIT)),
        ],
        compiler_params=pltpu.CompilerParams(
            collective_id=1, has_side_effects=True, vmem_limit_bytes=48 * 1024 * 1024
        ),
        name="experts",
    )(normed, kept, routes, w_gate, w_up, w_down)


def body(
    q_proj,
    key_projection,
    value_projection,
    segments,
    resid,
    norm_gain,
    route_ids,
    route_gates,
    w_gate,
    w_up,
    w_down,
):
    normed, kept, routes = attention_call(
        q_proj,
        key_projection,
        value_projection,
        segments.reshape(1, -1),
        resid,
        norm_gain.reshape(1, -1),
        jnp.tile(route_ids.T, (1, GROUP)),
        jnp.tile(route_gates.T, (1, GROUP)),
    )
    return expert_call(normed, kept, routes, w_gate, w_up, w_down)


def solution(mesh):
    n_cp, n_tp, n_dp = (mesh.shape[a] for a in ("cp", "tp", "dp"))
    fine = Mesh(
        mesh.devices.reshape(n_cp // 2, 2, n_tp // 2, 2, n_dp), ("z", "xh", "xl", "core", "dp")
    )
    cp, tp = ("z", "xh"), ("xl", "core")
    placed = (
        P(cp, tp + ("dp",)),
        P(cp, None),
        P(cp, None),
        P(),
        P(cp, tp + ("dp",)),
        P(),
        P(cp + ("dp",), None),
        P(cp + ("dp",), None),
        P(cp + ("dp",), tp, None),
        P(cp + ("dp",), tp, None),
        P(cp + ("dp",), None, tp),
    )
    return jax.shard_map(
        body, mesh=fine, in_specs=placed, out_specs=P(cp + ("dp",), tp), check_vma=False
    )
```

time: 450 us -> 160 us (0.36)
  waiting for transfers between devices: 287 us -> 0 us
  Pallas kernels: 0 us -> 147 us
  blocking collectives: 108 us -> 0 us
  matrix products: 15.6 us -> 0 us
  between operations: 13.4 us -> 0.04 us
  other arithmetic: 9.66 us -> 0 us
    all_gather x3 -> x0, waiting for transfers between devices: 208 us -> none  [the longest x1 152 us: attend(): lax.all_gather(jnp.concatenate([k_mine, v_mine], 1), ('z', 'xh'), axis=0,...]
    pallas_call x0 -> x2, Pallas kernels: none -> 147 us  [the longest x1 97.3 us: expert_call(): pl.pallas_call(functools.partial(expert_kernel, n), out_shape=jax.ShapeDt...]
    reduce_scatter x1 -> x0, waiting for transfers between devices: 73.6 us -> none  [body(): lax.psum_scatter(partial, 'z', scatter_dimension=0, tiled=False)]
    all_gather x3 -> x0, blocking collectives: 63.7 us -> none  [the longest x1 28.2 us: body(): ids = lax.all_gather(route_ids, 'z', axis=0)]
    all_to_all x2 -> x0, blocking collectives: 38.8 us -> none  [the longest x1 21.8 us: body(): lax.all_to_all(produced.reshape(plane, n_z * CAP, width), ('xh', 'dp'), s...]
    dot_general x7 -> x0, matrix products: 15.6 us -> none  [the longest x1 4.35 us: body(): lax.dot_general(full, w_gate[0], contract, preferred_element_type=jnp.flo...]
    unnamed x10 -> x17, local copies, waits for them, and re-layouts: 0.03 us -> 8.92 us
    reshape x7 -> x1, local copies, waits for them, and re-layouts: 8.8 us -> 0.71 us  [body(): norm_gain.reshape(1, -1)]
  transfers between devices with their start and end apart: 5 -> 0, of which waited for: 5 -> 0; matrix products, arithmetic and copies ran while one was open for 2% -> 0% of each run, Pallas kernels for 0% -> 0%
where the time goes in v2:
time: 160 us; the launch traced here: 159 us
  Pallas kernels  147 us (92%)
  local copies, waits for them, and re-layouts  11.2 us (7%)
    pallas_call x1, Pallas kernels, expert_call(): pl.pallas_call(functools.partial(expert_kernel, n), out_shape=jax.ShapeDt...  97.3 us
    pallas_call x1, Pallas kernels, attention_call(): pl.pallas_call(functools.partial(attention_kernel, n), out_shape=(jax.Sha...  50.2 us
    unnamed x17, local copies, waits for them, and re-layouts  8.92 us

profile of v2, /device:TPU:6, one launch (start us, length us, event | category | flops | bytes accessed | tf_op | source)
XLA Modules:
  0.0 158.7 jit_solution(10793055538943286341)
XLA Ops:
  0.0 0.7 reshape.15.gain_ref
  0.7 0.7 tile.8
  1.4 0.1 tile.9.ids_ref
  1.5 0.7 tile.20
  2.2 0.1 tile.21.gates_ref
  2.3 0.0 copy-start.3
  2.3 0.8 copy-done.3
  3.1 0.0 copy-start.4
  3.1 0.8 copy-done.4
  3.9 0.0 copy-start.5
  3.9 0.8 copy-done.5
  4.8 0.0 copy-start.6
  4.8 0.8 copy-done.6
  5.6 0.0 copy-start.7
  5.6 0.7 copy-done.7
  6.3 50.2 %attention.1 = (bf16[32,2048]{1,0:T(8,128)(2,1)S(1)}, bf16[32,1024]{1,0:T(8,128)(2,1)S(1)}, f32[16,2,8,128]{3,2,1,0:T(8,128)S(1)}) custom-call(bf16[128,256]{1,0:T(8,128)(2,1)S(1)} %copy-done.3, bf16[128,256]{1,0:T(8,128)(2,1)S(1)} %copy-done.4, bf16[128,256]{1,0:T(8,128)(2,1)S(1)} %copy-done.5, s32[1,4096]{1,0:T(1,128)S(1)} %bitcast.3, ...), custom_call_target="tpu_custom_call" | custom-call | tf_op jit(solution)/shard_map/attention/pallas_call | solution.py:265
  56.6 0.0 copy-start
  56.6 1.4 copy-done
  58.0 0.0 copy-start.1
  58.0 1.4 copy-done.1
  59.4 0.0 copy-start.2
  59.4 1.4 copy-done.2
  60.8 97.3 %experts.1 = bf16[32,1024]{1,0:T(8,128)(2,1)S(1)} custom-call(bf16[32,2048]{1,0:T(8,128)(2,1)S(1)} %get-tuple-element.8.normed_ref, bf16[32,1024]{1,0:T(8,128)(2,1)S(1)} %get-tuple-element.9.kept_ref, f32[16,2,8,128]{3,2,1,0:T(8,128)S(1)} %get-tuple-element.10.routes_ref, bf16[1,192,4096]{2,1,0:T(8,128)(2,1)S(1)} %copy-done, ...), custom_call_target="tpu_custom_call" | custom-call | tf_op jit(solution)/shard_map/experts/pallas_call | solution.py:557
  158.1 0.6 copy.13
Async XLA Ops:
  2.3 0.8 copy-start.3
  3.1 0.8 copy-start.4
  3.9 0.8 copy-start.5
  4.8 0.8 copy-start.6
  5.6 0.7 copy-start.7
  56.6 1.4 copy-start
  58.0 1.4 copy-start.1
  59.4 1.4 copy-start.2

commit v3 on v2

v3 whole, which is shorter than its diff:
```python
import functools

import jax
import jax.numpy as jnp
from jax import lax
from jax.experimental import pallas as pl
from jax.experimental.pallas import tpu as pltpu
from jax.sharding import Mesh, PartitionSpec as P

HEAD_WIDTH = 128
CAP = 4
REACH = 2048
BLOCK = 32
GROUP = 4
SLOTS = GROUP * CAP
SPLIT = 4
PIECES = 4
FAR_FIRST = True
PAIRED = 4
LAG_CORE, LAG_USE = 3, 2

epsilon = 1e-06
masked_score = -1e30
bf16, f32 = jnp.bfloat16, jnp.float32
MESH = pl.DeviceIdType.MESH


def sizes():
    return {a: lax.axis_size(a) for a in ("z", "xh", "xl", "core", "dp")}


def places():
    return {a: lax.axis_index(a) for a in ("z", "xh", "xl", "core", "dp")}


def moved(me, n, **steps):
    return {a: lax.rem(me[a] + n[a] + s, n[a]) for a, s in steps.items()}


def shifts(n, axes):
    found = [{}]
    for a in axes:
        found = [{**f, a: s} for f in found for s in range(n[a])]
    return found[1:]


def copy_to(src, dst, send, recv, device):
    return pltpu.make_async_remote_copy(
        src_ref=src, dst_ref=dst, send_sem=send, recv_sem=recv, device_id=device, device_id_type=MESH
    )


def greet(me, n, steps):
    barrier = pltpu.get_barrier_semaphore()
    for s in steps:
        pl.semaphore_signal(barrier, inc=1, device_id=moved(me, n, **s), device_id_type=MESH)
    pl.semaphore_wait(barrier, len(steps))


def next_stop(k):
    if k <= PAIRED:
        return k - 1
    return k - 2 if k % 2 == 0 else k - 1


def up_place(k):
    return 2 * k - 1 if k else 0


def layer_kernel(
    n, q_hbm, k_hbm, v_hbm, seg_hbm, resid_hbm, gain_hbm, ids_hbm, gates_hbm, w_gate_hbm, w_up_hbm, w_down_hbm,
    mixed_ref,
    q_ref, k_ref, v_ref, seg_ref, resid_ref, gain_ref, ids_ref, gates_ref, w_gate, w_up, w_down,
    kv, queries, table, routes, stage, fold, kept, wide_gain,
    tokens, picked, arrived, hidden, produced, returned, partial, fall_out, fall_in, rise_out, rise_in,
    in_sem, z_send, z_recv, plane_send, plane_recv, share_send, share_recv,
    route_send, route_recv, fold_send, fold_recv,
    up_send, up_recv, down_send, down_recv, pick_send, pick_recv, core_send, core_recv,
    hid_send, hid_recv, ret_send, ret_recv, fall_send, fall_recv, rise_send, rise_recv,
):
    me = places()
    rows = q_ref.shape[0]
    heads = q_ref.shape[1] // HEAD_WIDTH
    plane_rows = n["xh"] * rows
    reach = min(-(-REACH // plane_rows), n["z"] - 1)
    up, down = n["z"] // 2, n["z"] // 2 - 1
    groups = n["z"] // GROUP
    plane = shifts(n, ("xh", "dp"))
    group = shifts(n, ("xl", "core", "dp"))
    tensor_steps = shifts(n, ("xl", "core"))
    line = [{"z": s} for s in range(1, n["z"])]
    core = me["core"]
    tensor = me["xl"] * n["core"] + core
    mine = me["xh"] * n["dp"] + me["dp"]
    experts = n["xh"] * n["dp"]

    pairs = (
        (k_hbm, k_ref), (v_hbm, v_ref), (ids_hbm, ids_ref), (gates_hbm, gates_ref), (q_hbm, q_ref),
        (seg_hbm, seg_ref), (resid_hbm, resid_ref), (gain_hbm, gain_ref),
        (w_gate_hbm, w_gate), (w_up_hbm, w_up), (w_down_hbm, w_down),
    )
    loads = [pltpu.make_async_copy(a, b, in_sem.at[i]) for i, (a, b) in enumerate(pairs)]
    for c in loads:
        c.start()
    crossed = [{**p, "xl": n["xl"] // 2 if p["xh"] else 0} for p in plane]
    greet(
        me, n,
        line + plane + [g for g in group if g["xl"] or g["core"]] + [p for p in crossed if p["xl"]],
    )

    quarter = rows // n["dp"]
    start = pl.multiple_of(me["xh"] * rows + me["dp"] * quarter, quarter)
    here = pl.ds(start, quarter)
    head = pl.ds(pl.multiple_of(me["xl"] * HEAD_WIDTH, HEAD_WIDTH), HEAD_WIDTH)
    own = pl.ds(pl.multiple_of(me["dp"] * quarter, quarter), quarter)
    loads[0].wait()
    loads[1].wait()
    kv[core, 0, here, :] = jnp.where(core == 0, k_ref[own, head], v_ref[own, head])

    def z_copy(d):
        return copy_to(
            kv.at[core, 0, here], kv.at[core, d, here], z_send.at[d], z_recv.at[d], moved(me, n, z=d)
        )

    def plane_copy(d, i):
        return copy_to(
            kv.at[core, d, here], kv.at[core, d, here],
            plane_send.at[d, i], plane_recv.at[d, i], moved(me, n, **plane[i]),
        )

    def share_copy(d, which):
        return copy_to(
            kv.at[which, d], kv.at[which, d], share_send.at[d], share_recv.at[d], moved(me, n, core=1)
        )

    order = [0] + list(range(reach, 0, -1)) if FAR_FIRST else list(range(reach + 1))
    for d in order[1:]:
        z_copy(d).start()
    for i in range(len(plane)):
        plane_copy(0, i).start()

    lanes = table.shape[2]
    all_experts = table.shape[1]
    token = lax.broadcasted_iota(jnp.int32, (BLOCK, lanes), 0)
    lane = lax.broadcasted_iota(jnp.int32, (BLOCK, lanes), 1)
    spread = jnp.where(lax.rem(lane, BLOCK) == token, 1.0, 0.0)
    over = (((0,), (0,)), ((), ()))
    exact = dict(preferred_element_type=f32, precision=lax.Precision.HIGHEST)
    loads[2].wait()
    loads[3].wait()
    ids = jnp.dot(ids_ref[...].astype(f32), spread, **exact)
    gates = jnp.dot(gates_ref[...], spread, **exact)
    expert = lax.broadcasted_iota(jnp.int32, (all_experts, lanes), 0).astype(f32)
    named = jnp.zeros((all_experts, lanes), f32)
    weight = jnp.zeros((all_experts, lanes), f32)
    for j in range(ids.shape[0]):
        equal = jnp.abs(expert - ids[j : j + 1, :]) < 0.5
        named += jnp.where(equal, 1.0, 0.0)
        weight += jnp.where(equal, gates[j : j + 1, :], 0.0)
    earlier = lax.broadcasted_iota(jnp.int32, (lanes, lanes), 0)
    later = lax.broadcasted_iota(jnp.int32, (lanes, lanes), 1)
    before = (earlier < later) & (earlier // BLOCK == later // BLOCK)
    rank = jnp.dot(
        named.astype(bf16), jnp.where(before, 1.0, 0.0).astype(bf16), preferred_element_type=f32
    )
    table[0] = jnp.where(named > 0.5, rank, 2.0 * CAP)
    table[1] = weight

    def rows_of(plane_index):
        return pl.ds(pl.multiple_of(plane_index * experts, experts), experts)

    route_copies = []
    for k, place in [(k, 2 * k - 1) for k in range(1, up + 1)] + [(-k, 2 * k) for k in range(1, down + 1)]:
        target = moved(me, n, z=k)
        route_copies.append(
            copy_to(
                table.at[:, rows_of(target["z"])], routes.at[place],
                route_send.at[place], route_recv.at[place], target,
            )
        )
    routes[0] = table[:, rows_of(me["z"]), :]

    for c in loads[4:8]:
        c.wait()
    wide_gain[...] = gain_ref[...].astype(f32)
    for h in range(heads):
        queries[h * rows : (h + 1) * rows] = q_ref[:, h * HEAD_WIDTH : (h + 1) * HEAD_WIDTH]
    all_rows = heads * rows
    context = me["z"] * n["xh"] + me["xh"]
    first_row = pl.multiple_of(context * rows, rows)
    seg_here = seg_ref[:, pl.ds(first_row, rows)].astype(f32)
    r = lax.broadcasted_iota(jnp.int32, (all_rows, rows), 0)
    c = lax.broadcasted_iota(jnp.int32, (all_rows, rows), 1)
    seg_rows = jnp.sum(jnp.where(lax.rem(r, rows) == c, seg_here, 0.0), 1, keepdims=True)
    q_position = first_row + lax.rem(
        lax.broadcasted_iota(jnp.int32, (all_rows, plane_rows), 0), rows
    )
    k_offset = lax.broadcasted_iota(jnp.int32, (all_rows, plane_rows), 1)
    state = None
    for t in range(len(order) + LAG_CORE + LAG_USE):
        if 1 <= t < len(order):
            z_copy(order[t]).wait_recv()
            for i in range(len(plane)):
                plane_copy(order[t], i).start()
            if t == len(order) - 1:
                for copy in route_copies:
                    copy.start()
        if 0 <= t - LAG_CORE < len(order):
            for i in range(len(plane)):
                plane_copy(order[t - LAG_CORE], i).wait_recv()
            share_copy(order[t - LAG_CORE], core).start()
        if t < LAG_CORE + LAG_USE:
            continue
        d = order[t - LAG_CORE - LAG_USE]
        share_copy(d, 1 - core).wait_recv()
        first_key = pl.multiple_of(lax.rem(me["z"] + n["z"] - d, n["z"]) * plane_rows, plane_rows)
        scores = (
            lax.dot_general(
                queries[...], kv[0, d], (((1,), (1,)), ((), ())), preferred_element_type=f32
            )
            * HEAD_WIDTH ** (-0.5)
        )
        seg_keys = seg_ref[:, pl.ds(first_key, plane_rows)].astype(f32)
        allowed = (first_key + k_offset <= q_position) & (seg_keys == seg_rows)
        scores = jnp.where(allowed, scores, masked_score)
        top = jnp.max(scores, 1, keepdims=True)
        if state is None:
            weights = jnp.exp(scores - top)
            total = jnp.sum(weights, 1, keepdims=True)
            acc = jnp.dot(weights.astype(bf16), kv[1, d], preferred_element_type=f32)
        else:
            old_top, old_total, old_acc = state
            top = jnp.maximum(old_top, top)
            weights = jnp.exp(scores - top)
            fade = jnp.exp(old_top - top)
            total = old_total * fade + jnp.sum(weights, 1, keepdims=True)
            acc = old_acc * fade + jnp.dot(
                weights.astype(bf16), kv[1, d], preferred_element_type=f32
            )
        state = (top, total, acc)
    attended = state[2] / state[1]
    for h in range(heads):
        cols = slice(h * HEAD_WIDTH, (h + 1) * HEAD_WIDTH)
        stage[:, cols] = (
            resid_ref[:, cols].astype(f32) + attended[h * rows : (h + 1) * rows]
        ).astype(bf16)

    slab = tensor * n["dp"] + me["dp"]

    def rows_for(y):
        return pl.ds(pl.multiple_of(y * quarter, quarter), quarter)

    fold_copies = []
    for i, g in enumerate(group):
        target = moved(me, n, **g)
        fold_copies.append(
            copy_to(
                stage.at[rows_for(target["dp"])], fold.at[slab],
                fold_send.at[i], fold_recv.at[i], target,
            )
        )
        fold_copies[-1].start()
    fold[slab] = stage[rows_for(me["dp"]), :]
    for f in route_copies + fold_copies:
        f.wait_recv()
    slabs = fold.shape[0]
    width = stage.shape[1]
    squares = jnp.zeros((quarter, width), f32)
    for s in range(slabs):
        v = fold[s].astype(f32)
        squares += v * v
    squares = jnp.sum(squares, 1, keepdims=True)
    inverse = lax.rsqrt(squares / (slabs * width) + epsilon)
    per_core = slabs // n["core"]
    piece_width = tokens.shape[3]

    def up_copy(k, p):
        return copy_to(
            tokens.at[up_place(k), p], tokens.at[up_place(k + 1), p],
            up_send.at[k, p], up_recv.at[k, p], moved(me, n, z=1),
        )

    def down_copy(k, p):
        return copy_to(
            tokens.at[2 * k, p], tokens.at[2 * k + 2, p],
            down_send.at[k, p], down_recv.at[k, p], moved(me, n, z=-1),
        )

    for i in range(per_core):
        s = core * per_core + i
        lines = [wide_gain[pl.ds(s * (width // 128) + r, 1), :] for r in range(width // 128)]
        gain = jnp.concatenate(lines, 1)
        p, q = divmod(i * width, piece_width)
        tokens[0, p, :, q : q + width] = (fold[s].astype(f32) * inverse * gain).astype(bf16)
        if q + width == piece_width:
            up_copy(0, p).start()
            down_copy(0, p).start()
    for i in range(n["dp"]):
        kept[:, i * width : (i + 1) * width] = fold[tensor * n["dp"] + i]

    def pick_copy(g, i):
        to = moved(me, n, **crossed[i])
        return copy_to(
            picked.at[g, to["xh"] * n["dp"] + to["dp"]], arrived.at[core, g, mine],
            pick_send.at[g, i], pick_recv.at[g, i], to,
        )

    def core_copy(g, half):
        return copy_to(
            arrived.at[half, g], arrived.at[half, g],
            core_send.at[g], core_recv.at[g], moved(me, n, core=1),
        )

    def hid_copy(g, i):
        return copy_to(
            hidden.at[g, tensor], hidden.at[g, tensor],
            hid_send.at[g, i], hid_recv.at[g, i], moved(me, n, **tensor_steps[i]),
        )

    def ret_copy(g, i):
        to = moved(me, n, **{a: -s for a, s in plane[i].items()})
        return copy_to(
            produced.at[g, to["xh"] * n["dp"] + to["dp"]], returned.at[g, mine],
            ret_send.at[g, i], ret_recv.at[g, i], to,
        )

    def slots_of(g):
        lane = lax.broadcasted_iota(jnp.int32, (experts, lanes), 1)
        rank, weight = routes[GROUP * g, 0], routes[GROUP * g, 1]
        for j in range(1, GROUP):
            inside = lane // BLOCK == j
            rank = jnp.where(inside, routes[GROUP * g + j, 0], rank)
            weight = jnp.where(inside, routes[GROUP * g + j, 1], weight)
        shape = (experts, SLOTS, lanes)
        slot = lax.broadcasted_iota(jnp.int32, shape, 1)
        token = lax.broadcasted_iota(jnp.int32, shape, 2)
        held = (jnp.broadcast_to(rank[:, None, :], shape) == lax.rem(slot, CAP).astype(f32)) & (
            token // BLOCK == slot // CAP
        )
        weight = jnp.where(held, jnp.broadcast_to(weight[:, None, :], shape), 0.0)
        flat = (experts * SLOTS, lanes)
        return jnp.where(held, 1.0, 0.0).reshape(flat), weight.reshape(flat)

    def pick(g):
        chosen, _ = slots_of(g)
        chosen = chosen.astype(bf16)
        for p in range(PIECES):
            block = tokens[GROUP * g : GROUP * (g + 1), p].reshape(GROUP * BLOCK, piece_width)
            out = jnp.dot(chosen, block, preferred_element_type=f32).astype(bf16)
            picked[g, :, :, p * piece_width : (p + 1) * piece_width] = out.reshape(
                experts, SLOTS, piece_width
            )
        for i in range(len(plane)):
            pick_copy(g, i).start()
        arrived[core, g, mine] = picked[g, mine]

    def pass_on(g):
        for i in range(len(plane)):
            pick_copy(g, i).wait_recv()
        core_copy(g, core).start()

    contract = (((1,), (1,)), ((), ()))
    n_slots = experts * SLOTS

    def into_hidden(g):
        core_copy(g, 1 - core).wait_recv()
        gate_val = up_val = None
        half = arrived.shape[-1]
        for h in range(n["core"]):
            x = arrived[h, g].reshape(n_slots, half)
            cols = slice(h * half, (h + 1) * half)
            a = lax.dot_general(x, w_gate[0, :, cols], contract, preferred_element_type=f32)
            b = lax.dot_general(x, w_up[0, :, cols], contract, preferred_element_type=f32)
            gate_val = a if gate_val is None else gate_val + a
            up_val = b if up_val is None else up_val + b
        hidden[g, tensor] = (gate_val / (1.0 + jnp.exp(-gate_val)) * up_val).astype(bf16)
        for i in range(len(tensor_steps)):
            hid_copy(g, i).start()

    def out_of_hidden(g):
        for i in range(len(tensor_steps)):
            hid_copy(g, i).wait_recv()
        units = hidden.shape[-1]
        out = None
        for s in range(hidden.shape[1]):
            term = jnp.dot(
                hidden[g, s], w_down[0, s * units : (s + 1) * units, :], preferred_element_type=f32
            )
            out = term if out is None else out + term
        produced[g] = out.astype(bf16).reshape(produced.shape[1:])
        for i in range(len(plane)):
            ret_copy(g, i).start()
        returned[g, mine] = produced[g, mine]

    def mix(g):
        _, weight = slots_of(g)
        for i in range(len(plane)):
            ret_copy(g, i).wait_recv()
        high = weight.astype(bf16)
        low = (weight - high.astype(f32)).astype(bf16)
        back = returned[g].reshape(n_slots, returned.shape[-1])
        total = lax.dot_general(high, back, over, preferred_element_type=f32)
        total += lax.dot_general(low, back, over, preferred_element_type=f32)
        partial[GROUP * g : GROUP * (g + 1)] = total.reshape(GROUP, BLOCK, total.shape[-1])

    for c in loads[8:]:
        c.wait()
    agenda = []
    for g in range(groups):
        for delay, rank, act in ((2, 0, pick), (4, 1, pass_on), (7, 2, out_of_hidden), (5, 3, into_hidden)):
            agenda.append((2 * g + delay, rank, g, act))
    agenda.sort(key=lambda entry: entry[:3])

    def run(step):
        while agenda and (step is None or agenda[0][0] <= step):
            _, _, g, act = agenda.pop(0)
            act(g)

    for step in range(1, up + 1):
        for p in range(PIECES):
            up_copy(step - 1, p).wait_recv()
            if step < up:
                up_copy(step, p).start()
            if step <= down:
                down_copy(step - 1, p).wait_recv()
                if step < down:
                    down_copy(step, p).start()
        run(step)
    run(None)

    part_width = partial.shape[-1] // SPLIT

    def part(place, s):
        return partial[place, :, s * part_width : (s + 1) * part_width]

    def fall_copy(k, s):
        return copy_to(
            fall_out.at[k - 1, s], fall_in.at[k - 1, s],
            fall_send.at[k - 1, s], fall_recv.at[k - 1, s], moved(me, n, z=next_stop(k) - k),
        )

    def rise_copy(k, s):
        return copy_to(
            rise_out.at[k - 1, s], rise_in.at[k - 1, s],
            rise_send.at[k - 1, s], rise_recv.at[k - 1, s], moved(me, n, z=k - next_stop(k)),
        )

    mixed_groups = set()

    def need(place):
        if place // GROUP not in mixed_groups:
            mixed_groups.add(place // GROUP)
            mix(place // GROUP)

    def gathered(total, k, s, copy, buffer, farthest):
        for other in range(k + 1, farthest + 1):
            if next_stop(other) == k:
                copy(other, s).wait_recv()
                total = total + buffer[other - 1, s].astype(f32)
        return total

    for t in range(up):
        k, j = up - t, down - t
        need(2 * k - 1)
        if j >= 1:
            need(2 * j)
        for s in range(SPLIT):
            fall_out[k - 1, s] = gathered(part(2 * k - 1, s), k, s, fall_copy, fall_in, up).astype(bf16)
            fall_copy(k, s).start()
            if j >= 1:
                rise_out[j - 1, s] = gathered(part(2 * j, s), j, s, rise_copy, rise_in, down).astype(bf16)
                rise_copy(j, s).start()
        if t == 0:
            for g in range(groups - 1, -1, -1):
                need(GROUP * g)
    for s in range(SPLIT):
        cols = slice(s * part_width, (s + 1) * part_width)
        total = kept[:, cols].astype(f32) + part(0, s)
        total = gathered(total, 0, s, rise_copy, rise_in, down)
        mixed_ref[:, cols] = gathered(total, 0, s, fall_copy, fall_in, up).astype(bf16)

    for d in order:
        if d:
            z_copy(d).wait_send()
        for i in range(len(plane)):
            plane_copy(d, i).wait_send()
        share_copy(d, core).wait_send()
    for c in route_copies + fold_copies:
        c.wait_send()
    for p in range(PIECES):
        for k in range(up):
            up_copy(k, p).wait_send()
        for k in range(down):
            down_copy(k, p).wait_send()
    for g in range(groups):
        core_copy(g, core).wait_send()
        for i in range(len(plane)):
            pick_copy(g, i).wait_send()
            ret_copy(g, i).wait_send()
        for i in range(len(tensor_steps)):
            hid_copy(g, i).wait_send()
    for s in range(SPLIT):
        for k in range(1, up + 1):
            fall_copy(k, s).wait_send()
        for k in range(1, down + 1):
            rise_copy(k, s).wait_send()


def body(
    q_proj,
    key_projection,
    value_projection,
    segments,
    resid,
    norm_gain,
    route_ids,
    route_gates,
    w_gate,
    w_up,
    w_down,
):
    n = sizes()
    rows, width = q_proj.shape
    plane_rows = n["xh"] * rows
    reach = min(-(-REACH // plane_rows), n["z"] - 1)
    experts = n["xh"] * n["dp"]
    tensors = n["xl"] * n["core"]
    lanes = GROUP * BLOCK
    slabs = tensors * n["dp"]
    up, down = n["z"] // 2, max(n["z"] // 2 - 1, 1)
    groups = n["z"] // GROUP
    half = slabs * width // n["core"]
    out_width = n["dp"] * width
    units = w_gate.shape[1]
    n_slots = experts * SLOTS
    part_width = out_width // SPLIT
    args = (
        q_proj, key_projection, value_projection, segments.reshape(1, -1), resid, norm_gain.reshape(-1, 128),
        route_ids.T, route_gates.T, w_gate, w_up, w_down,
    )
    held = (0, 1, 2, 3, 4, 5, 6, 7, 8, 9, 10)
    buffers = [
        ((2, reach + 1, plane_rows, HEAD_WIDTH), bf16),
        ((rows * width // HEAD_WIDTH, HEAD_WIDTH), bf16),
        ((2, experts * n["z"], lanes), f32),
        ((n["z"], 2, experts, lanes), f32),
        ((rows, width), bf16),
        ((slabs, BLOCK, width), bf16),
        ((BLOCK, out_width), bf16),
        ((slabs * width // 128, 128), f32),
        ((n["z"], PIECES, BLOCK, half // PIECES), bf16),
        ((groups, experts, SLOTS, half), bf16),
        ((n["core"], groups, experts, SLOTS, half), bf16),
        ((groups, tensors, n_slots, units), bf16),
        ((groups, experts, SLOTS, out_width), bf16),
        ((groups, experts, SLOTS, out_width), bf16),
        ((n["z"], BLOCK, out_width), f32),
        ((up, SPLIT, BLOCK, part_width), bf16),
        ((up, SPLIT, BLOCK, part_width), bf16),
        ((down, SPLIT, BLOCK, part_width), bf16),
        ((down, SPLIT, BLOCK, part_width), bf16),
    ]
    semaphores = [
        (reach + 1,), (reach + 1, experts), (reach + 1,), (n["z"],), (slabs,),
        (up, PIECES), (down, PIECES), (groups, experts), (groups,), (groups, tensors), (groups, experts),
        (up, SPLIT), (down, SPLIT),
    ]
    dma = pltpu.SemaphoreType.DMA
    return pl.pallas_call(
        functools.partial(layer_kernel, n),
        out_shape=jax.ShapeDtypeStruct((BLOCK, out_width), bf16),
        in_specs=[pl.BlockSpec(memory_space=pl.ANY)] * len(args),
        out_specs=pl.BlockSpec(memory_space=pltpu.VMEM),
        scratch_shapes=[pltpu.VMEM(args[i].shape, args[i].dtype) for i in held]
        + [pltpu.VMEM(*b) for b in buffers]
        + [dma((len(args),))]
        + [dma(shape) for shape in semaphores for _ in range(2)],
        compiler_params=pltpu.CompilerParams(
            collective_id=0, has_side_effects=True, vmem_limit_bytes=56 * 1024 * 1024
        ),
        name="layer",
    )(*args)


def solution(mesh):
    n_cp, n_tp, n_dp = (mesh.shape[a] for a in ("cp", "tp", "dp"))
    fine = Mesh(
        mesh.devices.reshape(n_cp // 2, 2, n_tp // 2, 2, n_dp), ("z", "xh", "xl", "core", "dp")
    )
    cp, tp = ("z", "xh"), ("xl", "core")
    placed = (
        P(cp, tp + ("dp",)),
        P(cp, None),
        P(cp, None),
        P(),
        P(cp, tp + ("dp",)),
        P(),
        P(cp + ("dp",), None),
        P(cp + ("dp",), None),
        P(cp + ("dp",), tp, None),
        P(cp + ("dp",), tp, None),
        P(cp + ("dp",), None, tp),
    )
    return jax.shard_map(
        body, mesh=fine, in_specs=placed, out_specs=P(cp + ("dp",), tp), check_vma=False
    )
```

time: 160 us -> 134 us (0.84)
  Pallas kernels: 147 us -> 131 us
  local copies, waits for them, and re-layouts: 11.2 us -> 1.47 us
    pallas_call x2 -> x1, Pallas kernels: 147 us -> 131 us  [body(): pl.pallas_call(functools.partial(layer_kernel, n), out_shape=jax.ShapeDty...]
    unnamed x17 -> x1, local copies, waits for them, and re-layouts: 8.92 us -> 1.47 us
where the time goes in v3:
time: 134 us; the launch traced here: 133 us
  Pallas kernels  131 us (98%)
  local copies, waits for them, and re-layouts  1.47 us (1%)
    pallas_call x1, Pallas kernels, body(): pl.pallas_call(functools.partial(layer_kernel, n), out_shape=jax.ShapeDty...  131 us

profile of v3, /device:TPU:6, one launch (start us, length us, event | category | flops | bytes accessed | tf_op | source)
XLA Modules:
  0.0 132.9 jit_solution(4498308819593221905)
XLA Ops:
  0.0 131.4 %layer.1 = bf16[32,1024]{1,0:T(8,128)(2,1)} custom-call(bf16[128,256]{1,0:T(8,128)(2,1)} %q_hbm.1, bf16[128,256]{1,0:T(8,128)(2,1)} %k_hbm.1, bf16[128,256]{1,0:T(8,128)(2,1)} %v_hbm.1, s32[1,4096]{1,0:T(1,128)} %bitcast.4, bf16[128,256]{1,0:T(8,128)(2,1)} %resid_hbm.1, bf16[32,128]{1,0:T(8,128)(2,1)} %bitcast.5, s32[8,32]{1,0:T(8,128)} %bitcast.6, ...), custom_call_target="tpu_custom_call" | custom-call | tf_op jit(solution)/shard_map/layer/pallas_call | solution.py:569
  131.4 1.5 %copy.13 = bf16[32,1024]{1,0:T(8,128)(2,1)} copy(bf16[32,1024]{1,0:T(8,128)(2,1)} %layer.1) | data formatting | bytes 131072

commit v4 on v3

--- a/solution.py
+++ b/solution.py
@@ -15,9 +15,8 @@
 SLOTS = GROUP * CAP
 SPLIT = 4
 PIECES = 4
-FAR_FIRST = True
 PAIRED = 4
-LAG_CORE, LAG_USE = 3, 2
+LAG_CORE, LAG_USE = 5, 2
 
 epsilon = 1e-06
 masked_score = -1e30
@@ -54,7 +53,7 @@
     barrier = pltpu.get_barrier_semaphore()
     for s in steps:
         pl.semaphore_signal(barrier, inc=1, device_id=moved(me, n, **s), device_id_type=MESH)
-    pl.semaphore_wait(barrier, len(steps))
+    return lambda: pl.semaphore_wait(barrier, len(steps))
 
 
 def next_stop(k):
@@ -71,10 +70,10 @@
     n, q_hbm, k_hbm, v_hbm, seg_hbm, resid_hbm, gain_hbm, ids_hbm, gates_hbm, w_gate_hbm, w_up_hbm, w_down_hbm,
     mixed_ref,
     q_ref, k_ref, v_ref, seg_ref, resid_ref, gain_ref, ids_ref, gates_ref, w_gate, w_up, w_down,
-    kv, queries, table, routes, stage, fold, kept, wide_gain,
+    kv, queries, notes, mixer, stage, fold, kept, wide_gain,
     tokens, picked, arrived, hidden, produced, returned, partial, fall_out, fall_in, rise_out, rise_in,
     in_sem, z_send, z_recv, plane_send, plane_recv, share_send, share_recv,
-    route_send, route_recv, fold_send, fold_recv,
+    note_up_send, note_up_recv, note_down_send, note_down_recv, fold_send, fold_recv,
     up_send, up_recv, down_send, down_recv, pick_send, pick_recv, core_send, core_recv,
     hid_send, hid_recv, ret_send, ret_recv, fall_send, fall_recv, rise_send, rise_recv,
 ):
@@ -88,12 +87,19 @@
     plane = shifts(n, ("xh", "dp"))
     group = shifts(n, ("xl", "core", "dp"))
     tensor_steps = shifts(n, ("xl", "core"))
-    line = [{"z": s} for s in range(1, n["z"])]
+    near = -(-reach // 2)
+    stride = max(near, 2 if PAIRED < up else 1)
+    line = [{"z": s} for s in range(1, n["z"]) if min(s, n["z"] - s) <= stride]
     core = me["core"]
     tensor = me["xl"] * n["core"] + core
     mine = me["xh"] * n["dp"] + me["dp"]
     experts = n["xh"] * n["dp"]
 
+    crossed = [{**p, "xl": n["xl"] // 2 if p["xh"] else 0} for p in plane]
+    met = greet(
+        me, n,
+        line + plane + [g for g in group if g["xl"] or g["core"]] + [p for p in crossed if p["xl"]],
+    )
     pairs = (
         (k_hbm, k_ref), (v_hbm, v_ref), (ids_hbm, ids_ref), (gates_hbm, gates_ref), (q_hbm, q_ref),
         (seg_hbm, seg_ref), (resid_hbm, resid_ref), (gain_hbm, gain_ref),
@@ -102,11 +108,7 @@
     loads = [pltpu.make_async_copy(a, b, in_sem.at[i]) for i, (a, b) in enumerate(pairs)]
     for c in loads:
         c.start()
-    crossed = [{**p, "xl": n["xl"] // 2 if p["xh"] else 0} for p in plane]
-    greet(
-        me, n,
-        line + plane + [g for g in group if g["xl"] or g["core"]] + [p for p in crossed if p["xl"]],
-    )
+    met()
 
     quarter = rows // n["dp"]
     start = pl.multiple_of(me["xh"] * rows + me["dp"] * quarter, quarter)
@@ -118,8 +120,10 @@
     kv[core, 0, here, :] = jnp.where(core == 0, k_ref[own, head], v_ref[own, head])
 
     def z_copy(d):
-        return copy_to(
-            kv.at[core, 0, here], kv.at[core, d, here], z_send.at[d], z_recv.at[d], moved(me, n, z=d)
+        first = 0 if d <= near else near
+        return copy_to(
+            kv.at[core, first, here], kv.at[core, d, here],
+            z_send.at[d], z_recv.at[d], moved(me, n, z=d - first),
         )
 
     def plane_copy(d, i):
@@ -133,14 +137,13 @@
             kv.at[which, d], kv.at[which, d], share_send.at[d], share_recv.at[d], moved(me, n, core=1)
         )
 
-    order = [0] + list(range(reach, 0, -1)) if FAR_FIRST else list(range(reach + 1))
-    for d in order[1:]:
+    order = [0, near] + [d for d in range(1, reach + 1) if d != near]
+    for d in order[1 : near + 1]:
         z_copy(d).start()
     for i in range(len(plane)):
         plane_copy(0, i).start()
 
-    lanes = table.shape[2]
-    all_experts = table.shape[1]
+    lanes = notes.shape[-1]
     token = lax.broadcasted_iota(jnp.int32, (BLOCK, lanes), 0)
     lane = lax.broadcasted_iota(jnp.int32, (BLOCK, lanes), 1)
     spread = jnp.where(lax.rem(lane, BLOCK) == token, 1.0, 0.0)
@@ -148,37 +151,23 @@
     exact = dict(preferred_element_type=f32, precision=lax.Precision.HIGHEST)
     loads[2].wait()
     loads[3].wait()
-    ids = jnp.dot(ids_ref[...].astype(f32), spread, **exact)
-    gates = jnp.dot(gates_ref[...], spread, **exact)
-    expert = lax.broadcasted_iota(jnp.int32, (all_experts, lanes), 0).astype(f32)
-    named = jnp.zeros((all_experts, lanes), f32)
-    weight = jnp.zeros((all_experts, lanes), f32)
-    for j in range(ids.shape[0]):
-        equal = jnp.abs(expert - ids[j : j + 1, :]) < 0.5
-        named += jnp.where(equal, 1.0, 0.0)
-        weight += jnp.where(equal, gates[j : j + 1, :], 0.0)
-    earlier = lax.broadcasted_iota(jnp.int32, (lanes, lanes), 0)
-    later = lax.broadcasted_iota(jnp.int32, (lanes, lanes), 1)
-    before = (earlier < later) & (earlier // BLOCK == later // BLOCK)
-    rank = jnp.dot(
-        named.astype(bf16), jnp.where(before, 1.0, 0.0).astype(bf16), preferred_element_type=f32
-    )
-    table[0] = jnp.where(named > 0.5, rank, 2.0 * CAP)
-    table[1] = weight
-
-    def rows_of(plane_index):
-        return pl.ds(pl.multiple_of(plane_index * experts, experts), experts)
-
-    route_copies = []
-    for k, place in [(k, 2 * k - 1) for k in range(1, up + 1)] + [(-k, 2 * k) for k in range(1, down + 1)]:
-        target = moved(me, n, z=k)
-        route_copies.append(
-            copy_to(
-                table.at[:, rows_of(target["z"])], routes.at[place],
-                route_send.at[place], route_recv.at[place], target,
-            )
-        )
-    routes[0] = table[:, rows_of(me["z"]), :]
+    notes[0, 0] = jnp.dot(ids_ref[...].astype(f32), spread, **exact)
+    notes[0, 1] = jnp.dot(gates_ref[...], spread, **exact)
+
+    def note_up(k):
+        return copy_to(
+            notes.at[up_place(k)], notes.at[up_place(k + 1)],
+            note_up_send.at[k], note_up_recv.at[k], moved(me, n, z=1),
+        )
+
+    def note_down(k):
+        return copy_to(
+            notes.at[2 * k], notes.at[2 * k + 2],
+            note_down_send.at[k], note_down_recv.at[k], moved(me, n, z=-1),
+        )
+
+    note_up(0).start()
+    note_down(0).start()
 
     for c in loads[4:8]:
         c.wait()
@@ -200,11 +189,11 @@
     for t in range(len(order) + LAG_CORE + LAG_USE):
         if 1 <= t < len(order):
             z_copy(order[t]).wait_recv()
+            if order[t] == near:
+                for d in range(near + 1, reach + 1):
+                    z_copy(d).start()
             for i in range(len(plane)):
                 plane_copy(order[t], i).start()
-            if t == len(order) - 1:
-                for copy in route_copies:
-                    copy.start()
         if 0 <= t - LAG_CORE < len(order):
             for i in range(len(plane)):
                 plane_copy(order[t - LAG_CORE], i).wait_recv()
@@ -261,7 +250,7 @@
         )
         fold_copies[-1].start()
     fold[slab] = stage[rows_for(me["dp"]), :]
-    for f in route_copies + fold_copies:
+    for f in fold_copies:
         f.wait_recv()
     slabs = fold.shape[0]
     width = stage.shape[1]
@@ -325,12 +314,27 @@
         )
 
     def slots_of(g):
-        lane = lax.broadcasted_iota(jnp.int32, (experts, lanes), 1)
-        rank, weight = routes[GROUP * g, 0], routes[GROUP * g, 1]
+        row = lax.broadcasted_iota(jnp.int32, (lanes, lanes), 0)
+        column = lax.broadcasted_iota(jnp.int32, (lanes, lanes), 1)
+        before = (row < column) & (row // BLOCK == column // BLOCK)
+        lane = lax.broadcasted_iota(jnp.int32, notes.shape[2:], 1)
+        ids, gates = notes[GROUP * g, 0], notes[GROUP * g, 1]
         for j in range(1, GROUP):
             inside = lane // BLOCK == j
-            rank = jnp.where(inside, routes[GROUP * g + j, 0], rank)
-            weight = jnp.where(inside, routes[GROUP * g + j, 1], weight)
+            ids = jnp.where(inside, notes[GROUP * g + j, 0], ids)
+            gates = jnp.where(inside, notes[GROUP * g + j, 1], gates)
+        expert = me["z"] * experts + lax.broadcasted_iota(jnp.int32, (experts, lanes), 0)
+        expert = expert.astype(f32)
+        named = jnp.zeros((experts, lanes), f32)
+        weight = jnp.zeros((experts, lanes), f32)
+        for j in range(ids.shape[0]):
+            equal = jnp.abs(expert - ids[j : j + 1, :]) < 0.5
+            named += jnp.where(equal, 1.0, 0.0)
+            weight += jnp.where(equal, gates[j : j + 1, :], 0.0)
+        rank = jnp.dot(
+            named.astype(bf16), jnp.where(before, 1.0, 0.0).astype(bf16), preferred_element_type=f32
+        )
+        rank = jnp.where(named > 0.5, rank, 2.0 * CAP)
         shape = (experts, SLOTS, lanes)
         slot = lax.broadcasted_iota(jnp.int32, shape, 1)
         token = lax.broadcasted_iota(jnp.int32, shape, 2)
@@ -342,7 +346,7 @@
         return jnp.where(held, 1.0, 0.0).reshape(flat), weight.reshape(flat)
 
     def pick(g):
-        chosen, _ = slots_of(g)
+        chosen, mixer[g] = slots_of(g)
         chosen = chosen.astype(bf16)
         for p in range(PIECES):
             block = tokens[GROUP * g : GROUP * (g + 1), p].reshape(GROUP * BLOCK, piece_width)
@@ -369,8 +373,8 @@
         for h in range(n["core"]):
             x = arrived[h, g].reshape(n_slots, half)
             cols = slice(h * half, (h + 1) * half)
-            a = lax.dot_general(x, w_gate[0, :, cols], contract, preferred_element_type=f32)
-            b = lax.dot_general(x, w_up[0, :, cols], contract, preferred_element_type=f32)
+            a = lax.dot_general(w_gate[0, :, cols], x, contract, preferred_element_type=f32)
+            b = lax.dot_general(w_up[0, :, cols], x, contract, preferred_element_type=f32)
             gate_val = a if gate_val is None else gate_val + a
             up_val = b if up_val is None else up_val + b
         hidden[g, tensor] = (gate_val / (1.0 + jnp.exp(-gate_val)) * up_val).astype(bf16)
@@ -380,20 +384,15 @@
     def out_of_hidden(g):
         for i in range(len(tensor_steps)):
             hid_copy(g, i).wait_recv()
-        units = hidden.shape[-1]
-        out = None
-        for s in range(hidden.shape[1]):
-            term = jnp.dot(
-                hidden[g, s], w_down[0, s * units : (s + 1) * units, :], preferred_element_type=f32
-            )
-            out = term if out is None else out + term
+        units = hidden[g].reshape(w_down.shape[1], n_slots)
+        out = lax.dot_general(units, w_down[0], over, preferred_element_type=f32)
         produced[g] = out.astype(bf16).reshape(produced.shape[1:])
         for i in range(len(plane)):
             ret_copy(g, i).start()
         returned[g, mine] = produced[g, mine]
 
     def mix(g):
-        _, weight = slots_of(g)
+        weight = mixer[g]
         for i in range(len(plane)):
             ret_copy(g, i).wait_recv()
         high = weight.astype(bf16)
@@ -417,6 +416,13 @@
             act(g)
 
     for step in range(1, up + 1):
+        note_up(step - 1).wait_recv()
+        if step < up:
+            note_up(step).start()
+        if step <= down:
+            note_down(step - 1).wait_recv()
+            if step < down:
+                note_down(step).start()
         for p in range(PIECES):
             up_copy(step - 1, p).wait_recv()
             if step < up:
@@ -458,6 +464,32 @@
                 copy(other, s).wait_recv()
                 total = total + buffer[other - 1, s].astype(f32)
         return total
+
+    def settle():
+        for d in order:
+            if d:
+                z_copy(d).wait_send()
+            for i in range(len(plane)):
+                plane_copy(d, i).wait_send()
+            share_copy(d, core).wait_send()
+        for c in fold_copies:
+            c.wait_send()
+        for k in range(up):
+            note_up(k).wait_send()
+        for k in range(down):
+            note_down(k).wait_send()
+        for p in range(PIECES):
+            for k in range(up):
+                up_copy(k, p).wait_send()
+            for k in range(down):
+                down_copy(k, p).wait_send()
+        for g in range(groups):
+            core_copy(g, core).wait_send()
+            for i in range(len(plane)):
+                pick_copy(g, i).wait_send()
+                ret_copy(g, i).wait_send()
+            for i in range(len(tensor_steps)):
+                hid_copy(g, i).wait_send()
 
     for t in range(up):
         k, j = up - t, down - t
@@ -473,32 +505,13 @@
         if t == 0:
             for g in range(groups - 1, -1, -1):
                 need(GROUP * g)
+            settle()
     for s in range(SPLIT):
         cols = slice(s * part_width, (s + 1) * part_width)
         total = kept[:, cols].astype(f32) + part(0, s)
         total = gathered(total, 0, s, rise_copy, rise_in, down)
         mixed_ref[:, cols] = gathered(total, 0, s, fall_copy, fall_in, up).astype(bf16)
 
-    for d in order:
-        if d:
-            z_copy(d).wait_send()
-        for i in range(len(plane)):
-            plane_copy(d, i).wait_send()
-        share_copy(d, core).wait_send()
-    for c in route_copies + fold_copies:
-        c.wait_send()
-    for p in range(PIECES):
-        for k in range(up):
-            up_copy(k, p).wait_send()
-        for k in range(down):
-            down_copy(k, p).wait_send()
-    for g in range(groups):
-        core_copy(g, core).wait_send()
-        for i in range(len(plane)):
-            pick_copy(g, i).wait_send()
-            ret_copy(g, i).wait_send()
-        for i in range(len(tensor_steps)):
-            hid_copy(g, i).wait_send()
     for s in range(SPLIT):
         for k in range(1, up + 1):
             fall_copy(k, s).wait_send()
@@ -542,8 +555,8 @@
     buffers = [
         ((2, reach + 1, plane_rows, HEAD_WIDTH), bf16),
         ((rows * width // HEAD_WIDTH, HEAD_WIDTH), bf16),
-        ((2, experts * n["z"], lanes), f32),
-        ((n["z"], 2, experts, lanes), f32),
+        ((n["z"], 2, route_ids.shape[1], lanes), f32),
+        ((groups, n_slots, lanes), f32),
         ((rows, width), bf16),
         ((slabs, BLOCK, width), bf16),
         ((BLOCK, out_width), bf16),
@@ -551,7 +564,7 @@
         ((n["z"], PIECES, BLOCK, half // PIECES), bf16),
         ((groups, experts, SLOTS, half), bf16),
         ((n["core"], groups, experts, SLOTS, half), bf16),
-        ((groups, tensors, n_slots, units), bf16),
+        ((groups, tensors, units, n_slots), bf16),
         ((groups, experts, SLOTS, out_width), bf16),
         ((groups, experts, SLOTS, out_width), bf16),
         ((n["z"], BLOCK, out_width), f32),
@@ -561,7 +574,7 @@
         ((down, SPLIT, BLOCK, part_width), bf16),
     ]
     semaphores = [
-        (reach + 1,), (reach + 1, experts), (reach + 1,), (n["z"],), (slabs,),
+        (reach + 1,), (reach + 1, experts), (reach + 1,), (up,), (down,), (slabs,),
         (up, PIECES), (down, PIECES), (groups, experts), (groups,), (groups, tensors), (groups, experts),
         (up, SPLIT), (down, SPLIT),
     ]

time: 134 us -> 126 us (0.940)
  Pallas kernels: 131 us -> 123 us
    pallas_call x1, Pallas kernels: 131 us -> 123 us  [body(): pl.pallas_call(functools.partial(layer_kernel, n), out_shape=jax.ShapeDty...]
where the time goes in v4:
time: 126 us; the launch traced here: 125 us
  Pallas kernels  123 us (98%)
  local copies, waits for them, and re-layouts  1.47 us (1%)
    pallas_call x1, Pallas kernels, body(): pl.pallas_call(functools.partial(layer_kernel, n), out_shape=jax.ShapeDty...  123 us

profile of v4, /device:TPU:6, one launch (start us, length us, event | category | flops | bytes accessed | tf_op | source)
XLA Modules:
  0.0 124.6 jit_solution(588948953817332037)
XLA Ops:
  0.0 123.1 %layer.1 = bf16[32,1024]{1,0:T(8,128)(2,1)} custom-call(bf16[128,256]{1,0:T(8,128)(2,1)} %q_hbm.1, bf16[128,256]{1,0:T(8,128)(2,1)} %k_hbm.1, bf16[128,256]{1,0:T(8,128)(2,1)} %v_hbm.1, s32[1,4096]{1,0:T(1,128)} %bitcast.4, bf16[128,256]{1,0:T(8,128)(2,1)} %resid_hbm.1, bf16[32,128]{1,0:T(8,128)(2,1)} %bitcast.5, s32[8,32]{1,0:T(8,128)} %bitcast.6, ...), custom_call_target="tpu_custom_call" | custom-call | tf_op jit(solution)/shard_map/layer/pallas_call | solution.py:582
  123.1 1.5 %copy.13 = bf16[32,1024]{1,0:T(8,128)(2,1)} copy(bf16[32,1024]{1,0:T(8,128)(2,1)} %layer.1) | data formatting | bytes 131072

commit v5 on v4

--- a/solution.py
+++ b/solution.py
@@ -12,10 +12,11 @@
 REACH = 2048
 BLOCK = 32
 GROUP = 4
+HALF = GROUP // 2
 SLOTS = GROUP * CAP
 SPLIT = 4
 PIECES = 4
-PAIRED = 4
+PASS_LAG = 3
 LAG_CORE, LAG_USE = 5, 2
 
 epsilon = 1e-06
@@ -56,10 +57,13 @@
     return lambda: pl.semaphore_wait(barrier, len(steps))
 
 
-def next_stop(k):
-    if k <= PAIRED:
-        return k - 1
-    return k - 2 if k % 2 == 0 else k - 1
+def stops(far, late, meet):
+    if late <= 1:
+        return {k: k - 1 for k in range(1, far + 1)}
+    found = {k: k - 1 for k in range(1, far + 1)}
+    found[late] = meet
+    found[meet] = 0
+    return found
 
 
 def up_place(k):
@@ -70,7 +74,7 @@
     n, q_hbm, k_hbm, v_hbm, seg_hbm, resid_hbm, gain_hbm, ids_hbm, gates_hbm, w_gate_hbm, w_up_hbm, w_down_hbm,
     mixed_ref,
     q_ref, k_ref, v_ref, seg_ref, resid_ref, gain_ref, ids_ref, gates_ref, w_gate, w_up, w_down,
-    kv, queries, notes, mixer, stage, fold, kept, wide_gain,
+    kv, queries, notes, stage, fold, kept, wide_gain,
     tokens, picked, arrived, hidden, produced, returned, partial, fall_out, fall_in, rise_out, rise_in,
     in_sem, z_send, z_recv, plane_send, plane_recv, share_send, share_recv,
     note_up_send, note_up_recv, note_down_send, note_down_recv, fold_send, fold_recv,
@@ -88,8 +92,7 @@
     group = shifts(n, ("xl", "core", "dp"))
     tensor_steps = shifts(n, ("xl", "core"))
     near = -(-reach // 2)
-    stride = max(near, 2 if PAIRED < up else 1)
-    line = [{"z": s} for s in range(1, n["z"]) if min(s, n["z"] - s) <= stride]
+    line = [{"z": s} for s in range(1, n["z"]) if min(s, n["z"] - s) <= near]
     core = me["core"]
     tensor = me["xl"] * n["core"] + core
     mine = me["xh"] * n["dp"] + me["dp"]
@@ -313,16 +316,16 @@
             ret_send.at[g, i], ret_recv.at[g, i], to,
         )
 
-    def slots_of(g):
+    def slots_of(first, count):
         row = lax.broadcasted_iota(jnp.int32, (lanes, lanes), 0)
         column = lax.broadcasted_iota(jnp.int32, (lanes, lanes), 1)
         before = (row < column) & (row // BLOCK == column // BLOCK)
         lane = lax.broadcasted_iota(jnp.int32, notes.shape[2:], 1)
-        ids, gates = notes[GROUP * g, 0], notes[GROUP * g, 1]
-        for j in range(1, GROUP):
+        ids, gates = notes[first, 0], notes[first, 1]
+        for j in range(1, count):
             inside = lane // BLOCK == j
-            ids = jnp.where(inside, notes[GROUP * g + j, 0], ids)
-            gates = jnp.where(inside, notes[GROUP * g + j, 1], gates)
+            ids = jnp.where(inside, notes[first + j, 0], ids)
+            gates = jnp.where(inside, notes[first + j, 1], gates)
         expert = me["z"] * experts + lax.broadcasted_iota(jnp.int32, (experts, lanes), 0)
         expert = expert.astype(f32)
         named = jnp.zeros((experts, lanes), f32)
@@ -335,28 +338,31 @@
             named.astype(bf16), jnp.where(before, 1.0, 0.0).astype(bf16), preferred_element_type=f32
         )
         rank = jnp.where(named > 0.5, rank, 2.0 * CAP)
-        shape = (experts, SLOTS, lanes)
+        shape = (experts, count * CAP, lanes)
         slot = lax.broadcasted_iota(jnp.int32, shape, 1)
         token = lax.broadcasted_iota(jnp.int32, shape, 2)
         held = (jnp.broadcast_to(rank[:, None, :], shape) == lax.rem(slot, CAP).astype(f32)) & (
             token // BLOCK == slot // CAP
         )
         weight = jnp.where(held, jnp.broadcast_to(weight[:, None, :], shape), 0.0)
-        flat = (experts * SLOTS, lanes)
+        flat = (experts * count * CAP, lanes)
         return jnp.where(held, 1.0, 0.0).reshape(flat), weight.reshape(flat)
 
-    def pick(g):
-        chosen, mixer[g] = slots_of(g)
-        chosen = chosen.astype(bf16)
-        for p in range(PIECES):
-            block = tokens[GROUP * g : GROUP * (g + 1), p].reshape(GROUP * BLOCK, piece_width)
-            out = jnp.dot(chosen, block, preferred_element_type=f32).astype(bf16)
-            picked[g, :, :, p * piece_width : (p + 1) * piece_width] = out.reshape(
-                experts, SLOTS, piece_width
-            )
+    def pick(q):
+        chosen, _ = slots_of(HALF * q, HALF)
+        chosen = chosen[:, : HALF * BLOCK].astype(bf16)
+
+        def taken(p):
+            block = tokens[HALF * q : HALF * (q + 1), p].reshape(HALF * BLOCK, piece_width)
+            out = jnp.dot(chosen, block, preferred_element_type=f32)
+            return out.reshape(experts, HALF * CAP, piece_width)
+
+        for p in range(PIECES // 2):
+            both = jnp.concatenate([taken(p), taken(p + PIECES // 2)], 1)
+            picked[q, :, :, p * piece_width : (p + 1) * piece_width] = both.astype(bf16)
         for i in range(len(plane)):
-            pick_copy(g, i).start()
-        arrived[core, g, mine] = picked[g, mine]
+            pick_copy(q, i).start()
+        arrived[core, q, mine] = picked[q, mine]
 
     def pass_on(g):
         for i in range(len(plane)):
@@ -367,16 +373,23 @@
     n_slots = experts * SLOTS
 
     def into_hidden(g):
-        core_copy(g, 1 - core).wait_recv()
+        parts = range(HALF * g, HALF * (g + 1))
+        for q in parts:
+            core_copy(q, 1 - core).wait_recv()
         gate_val = up_val = None
-        half = arrived.shape[-1]
+        span = arrived.shape[-1]
         for h in range(n["core"]):
-            x = arrived[h, g].reshape(n_slots, half)
-            cols = slice(h * half, (h + 1) * half)
-            a = lax.dot_general(w_gate[0, :, cols], x, contract, preferred_element_type=f32)
-            b = lax.dot_general(w_up[0, :, cols], x, contract, preferred_element_type=f32)
-            gate_val = a if gate_val is None else gate_val + a
-            up_val = b if up_val is None else up_val + b
+            values = [arrived[h, q].astype(f32) for q in parts]
+            for r in range(2):
+                rows_here = slice(r * HALF * CAP, (r + 1) * HALF * CAP)
+                x = jnp.concatenate(
+                    [v[:, rows_here].reshape(experts * HALF * CAP, span) for v in values], 0
+                ).astype(bf16)
+                cols = slice((2 * h + r) * span, (2 * h + r + 1) * span)
+                a = lax.dot_general(w_gate[0, :, cols], x, contract, preferred_element_type=f32)
+                b = lax.dot_general(w_up[0, :, cols], x, contract, preferred_element_type=f32)
+                gate_val = a if gate_val is None else gate_val + a
+                up_val = b if up_val is None else up_val + b
         hidden[g, tensor] = (gate_val / (1.0 + jnp.exp(-gate_val)) * up_val).astype(bf16)
         for i in range(len(tensor_steps)):
             hid_copy(g, i).start()
@@ -386,13 +399,14 @@
             hid_copy(g, i).wait_recv()
         units = hidden[g].reshape(w_down.shape[1], n_slots)
         out = lax.dot_general(units, w_down[0], over, preferred_element_type=f32)
-        produced[g] = out.astype(bf16).reshape(produced.shape[1:])
+        out = out.reshape(2, experts, HALF * CAP, out.shape[-1])
+        produced[g] = jnp.concatenate([out[0], out[1]], 1).astype(bf16)
         for i in range(len(plane)):
             ret_copy(g, i).start()
         returned[g, mine] = produced[g, mine]
 
     def mix(g):
-        weight = mixer[g]
+        _, weight = slots_of(GROUP * g, GROUP)
         for i in range(len(plane)):
             ret_copy(g, i).wait_recv()
         high = weight.astype(bf16)
@@ -406,8 +420,11 @@
         c.wait()
     agenda = []
     for g in range(groups):
-        for delay, rank, act in ((2, 0, pick), (4, 1, pass_on), (7, 2, out_of_hidden), (5, 3, into_hidden)):
-            agenda.append((2 * g + delay, rank, g, act))
+        for delay, rank, act in ((6, 2, out_of_hidden), (5, 3, into_hidden)):
+            if act is into_hidden or g < groups - 1:
+                agenda.append((2 * g + delay, rank, g, act))
+        for q in range(2 * g, 2 * g + 2):
+            agenda += [(q + 1, 0, q, pick), (q + PASS_LAG, 1, q, pass_on)]
     agenda.sort(key=lambda entry: entry[:3])
 
     def run(step):
@@ -433,8 +450,19 @@
                     down_copy(step, p).start()
         run(step)
     run(None)
+    for g in range(groups - 2):
+        mix(g)
+    out_of_hidden(groups - 1)
+    if groups > 1:
+        mix(groups - 2)
 
     part_width = partial.shape[-1] // SPLIT
+    last = GROUP * (groups - 1)
+    fall_late, rise_late = last // 2 + 1, max(last // 2, 1)
+    if groups == 1:
+        fall_late = rise_late = 1
+    fall_meet, rise_meet = min(near, fall_late) - 1, min(near, rise_late) - 1
+    fall_stops, rise_stops = stops(up, fall_late, fall_meet), stops(down, rise_late, rise_meet)
 
     def part(place, s):
         return partial[place, :, s * part_width : (s + 1) * part_width]
@@ -442,28 +470,14 @@
     def fall_copy(k, s):
         return copy_to(
             fall_out.at[k - 1, s], fall_in.at[k - 1, s],
-            fall_send.at[k - 1, s], fall_recv.at[k - 1, s], moved(me, n, z=next_stop(k) - k),
+            fall_send.at[k - 1, s], fall_recv.at[k - 1, s], moved(me, n, z=fall_stops[k] - k),
         )
 
     def rise_copy(k, s):
         return copy_to(
             rise_out.at[k - 1, s], rise_in.at[k - 1, s],
-            rise_send.at[k - 1, s], rise_recv.at[k - 1, s], moved(me, n, z=k - next_stop(k)),
-        )
-
-    mixed_groups = set()
-
-    def need(place):
-        if place // GROUP not in mixed_groups:
-            mixed_groups.add(place // GROUP)
-            mix(place // GROUP)
-
-    def gathered(total, k, s, copy, buffer, farthest):
-        for other in range(k + 1, farthest + 1):
-            if next_stop(other) == k:
-                copy(other, s).wait_recv()
-                total = total + buffer[other - 1, s].astype(f32)
-        return total
+            rise_send.at[k - 1, s], rise_recv.at[k - 1, s], moved(me, n, z=k - rise_stops[k]),
+        )
 
     def settle():
         for d in order:
@@ -483,34 +497,61 @@
                 up_copy(k, p).wait_send()
             for k in range(down):
                 down_copy(k, p).wait_send()
+        for q in range(2 * groups):
+            core_copy(q, core).wait_send()
+            for i in range(len(plane)):
+                pick_copy(q, i).wait_send()
         for g in range(groups):
-            core_copy(g, core).wait_send()
             for i in range(len(plane)):
-                pick_copy(g, i).wait_send()
                 ret_copy(g, i).wait_send()
             for i in range(len(tensor_steps)):
                 hid_copy(g, i).wait_send()
 
-    for t in range(up):
-        k, j = up - t, down - t
-        need(2 * k - 1)
-        if j >= 1:
-            need(2 * j)
+    def gathered(total, k, s, copy, buffer, where):
+        for other in sorted(where):
+            if where[other] == k:
+                copy(other, s).wait_recv()
+                total = total + buffer[other - 1, s].astype(f32)
+        return total
+
+    def fall(k):
         for s in range(SPLIT):
-            fall_out[k - 1, s] = gathered(part(2 * k - 1, s), k, s, fall_copy, fall_in, up).astype(bf16)
+            total = gathered(part(2 * k - 1, s), k, s, fall_copy, fall_in, fall_stops)
+            fall_out[k - 1, s] = total.astype(bf16)
             fall_copy(k, s).start()
-            if j >= 1:
-                rise_out[j - 1, s] = gathered(part(2 * j, s), j, s, rise_copy, rise_in, down).astype(bf16)
-                rise_copy(j, s).start()
-        if t == 0:
-            for g in range(groups - 1, -1, -1):
-                need(GROUP * g)
-            settle()
+
+    def rise(k):
+        for s in range(SPLIT):
+            total = gathered(part(2 * k, s), k, s, rise_copy, rise_in, rise_stops)
+            rise_out[k - 1, s] = total.astype(bf16)
+            rise_copy(k, s).start()
+
+    def in_turn(*lines):
+        for i in range(max(len(ks) for _, ks in lines)):
+            for act, ks in lines:
+                if i < len(ks):
+                    act(ks[i])
+
+    def back_from(high, low):
+        return list(range(high, low, -1))
+
+    in_turn(
+        (fall, back_from(fall_late - 1, fall_meet)),
+        (rise, back_from(rise_late - 1, rise_meet)),
+        (fall, back_from(fall_meet - 1, 0)),
+        (rise, back_from(rise_meet - 1, 0)),
+    )
+    mix(groups - 1)
+    fall_last = back_from(up, fall_late - 1) + [fall_meet] * (fall_meet > 0)
+    rise_last = back_from(down, rise_late - 1) + [rise_meet] * (rise_meet > 0)
+    in_turn((fall, fall_last[:1]), (rise, rise_last[:1]))
+    settle()
+    in_turn((fall, fall_last[1:]), (rise, rise_last[1:]))
     for s in range(SPLIT):
         cols = slice(s * part_width, (s + 1) * part_width)
         total = kept[:, cols].astype(f32) + part(0, s)
-        total = gathered(total, 0, s, rise_copy, rise_in, down)
-        mixed_ref[:, cols] = gathered(total, 0, s, fall_copy, fall_in, up).astype(bf16)
+        total = gathered(total, 0, s, rise_copy, rise_in, rise_stops)
+        mixed_ref[:, cols] = gathered(total, 0, s, fall_copy, fall_in, fall_stops).astype(bf16)
 
     for s in range(SPLIT):
         for k in range(1, up + 1):
@@ -556,14 +597,13 @@
         ((2, reach + 1, plane_rows, HEAD_WIDTH), bf16),
         ((rows * width // HEAD_WIDTH, HEAD_WIDTH), bf16),
         ((n["z"], 2, route_ids.shape[1], lanes), f32),
-        ((groups, n_slots, lanes), f32),
         ((rows, width), bf16),
         ((slabs, BLOCK, width), bf16),
         ((BLOCK, out_width), bf16),
         ((slabs * width // 128, 128), f32),
         ((n["z"], PIECES, BLOCK, half // PIECES), bf16),
-        ((groups, experts, SLOTS, half), bf16),
-        ((n["core"], groups, experts, SLOTS, half), bf16),
+        ((2 * groups, experts, SLOTS, half // 2), bf16),
+        ((n["core"], 2 * groups, experts, SLOTS, half // 2), bf16),
         ((groups, tensors, units, n_slots), bf16),
         ((groups, experts, SLOTS, out_width), bf16),
         ((groups, experts, SLOTS, out_width), bf16),
@@ -575,7 +615,7 @@
     ]
     semaphores = [
         (reach + 1,), (reach + 1, experts), (reach + 1,), (up,), (down,), (slabs,),
-        (up, PIECES), (down, PIECES), (groups, experts), (groups,), (groups, tensors), (groups, experts),
+        (up, PIECES), (down, PIECES), (2 * groups, experts), (2 * groups,), (groups, tensors), (groups, experts),
         (up, SPLIT), (down, SPLIT),
     ]
     dma = pltpu.SemaphoreType.DMA

time: 126 us -> 118 us (0.937)
  Pallas kernels: 123 us -> 116 us
    pallas_call x1, Pallas kernels: 123 us -> 116 us  [body(): pl.pallas_call(functools.partial(layer_kernel, n), out_shape=jax.ShapeDty...]
where the time goes in v5:
time: 118 us
  Pallas kernels  116 us (98%)
  local copies, waits for them, and re-layouts  1.47 us (1%)
    pallas_call x1, Pallas kernels, body(): pl.pallas_call(functools.partial(layer_kernel, n), out_shape=jax.ShapeDty...  116 us

profile of v5, /device:TPU:6, one launch (start us, length us, event | category | flops | bytes accessed | tf_op | source)
XLA Modules:
  0.0 117.6 jit_solution(9505049157585422641)
XLA Ops:
  0.0 116.1 %layer.1 = bf16[32,1024]{1,0:T(8,128)(2,1)} custom-call(bf16[128,256]{1,0:T(8,128)(2,1)} %q_hbm.1, bf16[128,256]{1,0:T(8,128)(2,1)} %k_hbm.1, bf16[128,256]{1,0:T(8,128)(2,1)} %v_hbm.1, s32[1,4096]{1,0:T(1,128)} %bitcast.4, bf16[128,256]{1,0:T(8,128)(2,1)} %resid_hbm.1, bf16[32,128]{1,0:T(8,128)(2,1)} %bitcast.5, s32[8,32]{1,0:T(8,128)} %bitcast.6, ...), custom_call_target="tpu_custom_call" | custom-call | tf_op jit(solution)/shard_map/layer/pallas_call | solution.py:622
  116.1 1.5 %copy.13 = bf16[32,1024]{1,0:T(8,128)(2,1)} copy(bf16[32,1024]{1,0:T(8,128)(2,1)} %layer.1) | data formatting | bytes 131072

commit v6 on v5

--- a/solution.py
+++ b/solution.py
@@ -41,7 +41,8 @@
     found = [{}]
     for a in axes:
         found = [{**f, a: s} for f in found for s in range(n[a])]
-    return found[1:]
+    links = {"xh": 2, "xl": 1, "dp": 1, "core": 0}
+    return sorted(found[1:], key=lambda f: -sum(links[a] * min(s, n[a] - s) for a, s in f.items()))
 
 
 def copy_to(src, dst, send, recv, device):
@@ -407,10 +408,10 @@
 
     def mix(g):
         _, weight = slots_of(GROUP * g, GROUP)
+        high = weight.astype(bf16)
+        low = (weight - high.astype(f32)).astype(bf16)
         for i in range(len(plane)):
             ret_copy(g, i).wait_recv()
-        high = weight.astype(bf16)
-        low = (weight - high.astype(f32)).astype(bf16)
         back = returned[g].reshape(n_slots, returned.shape[-1])
         total = lax.dot_general(high, back, over, preferred_element_type=f32)
         total += lax.dot_general(low, back, over, preferred_element_type=f32)

time: 118 us -> 116 us (0.983)
  Pallas kernels: 116 us -> 113 us
    pallas_call x1, Pallas kernels: 116 us -> 113 us  [body(): pl.pallas_call(functools.partial(layer_kernel, n), out_shape=jax.ShapeDty...]
where the time goes in v6:
time: 116 us; the launch traced here: 115 us
  Pallas kernels  113 us (97%)
  local copies, waits for them, and re-layouts  1.47 us (1%)
    pallas_call x1, Pallas kernels, body(): pl.pallas_call(functools.partial(layer_kernel, n), out_shape=jax.ShapeDty...  113 us

profile of v6, /device:TPU:6, one launch (start us, length us, event | category | flops | bytes accessed | tf_op | source)
XLA Modules:
  0.0 114.6 jit_solution(6850699192488609823)
XLA Ops:
  0.0 113.1 %layer.1 = bf16[32,1024]{1,0:T(8,128)(2,1)} custom-call(bf16[128,256]{1,0:T(8,128)(2,1)} %q_hbm.1, bf16[128,256]{1,0:T(8,128)(2,1)} %k_hbm.1, bf16[128,256]{1,0:T(8,128)(2,1)} %v_hbm.1, s32[1,4096]{1,0:T(1,128)} %bitcast.4, bf16[128,256]{1,0:T(8,128)(2,1)} %resid_hbm.1, bf16[32,128]{1,0:T(8,128)(2,1)} %bitcast.5, s32[8,32]{1,0:T(8,128)} %bitcast.6, ...), custom_call_target="tpu_custom_call" | custom-call | tf_op jit(solution)/shard_map/layer/pallas_call | solution.py:623
  113.1 1.5 %copy.13 = bf16[32,1024]{1,0:T(8,128)(2,1)} copy(bf16[32,1024]{1,0:T(8,128)(2,1)} %layer.1) | data formatting | bytes 131072
